TPU v7x, 32 devices: a whole 2x2x4 slice. The times are simulated.
32 devices in a mesh: frames: 4 (over x, core), rows: 8 (over z, y).
Axes of the slice: x: 2, y: 2, z: 4, core: 2. Of those that a mesh axis runs over, the one named last changes fastest.
Arguments:
- clip_in: bfloat16 [16, 32, 64, 256], P('frames', 'rows'), may hold values from -6 to 6
- kernel_one: bfloat16 [3, 3, 3, 64, 64], replicated, may hold values from -0.15625 to 0.15625
- bias_one: float32 [64], replicated, may hold values from -3 to 3
- kernel_two: bfloat16 [3, 3, 3, 64, 64], replicated, may hold values from -0.3125 to 0.3125
- cotangent: bfloat16 [16, 32, 64, 256], P('frames', 'rows'), may hold values from -6 to 6
Outputs:
- block_out: bfloat16 [16, 32, 64, 256], P('frames', 'rows')
- grad_input: bfloat16 [16, 32, 64, 256], P('frames', 'rows')
- grad_first: float32 [3, 3, 3, 64, 64], replicated
- grad_second: float32 [3, 3, 3, 64, 64], replicated
- grad_bias: float32 [64], replicated
All inputs are finite; a program needn't handle non-finite values.
Results may differ from a plain program's by a relative error of at most 0.0065.
Values may be sent and summed in bfloat16 or wider, within the bound.
A program may use at most 64 MiB of HBM per device.

v0:
```python
import math

import jax
import jax.numpy as jnp
from jax import lax
from jax.sharding import PartitionSpec as P


def with_halo(block, sides, width):
    for axis, dim in sides:
        count = lax.axis_size(axis)
        forward = [(i, i + 1) for i in range(count - 1)]
        backward = [(target, source) for source, target in forward]
        low = lax.ppermute(
            lax.slice_in_dim(block, block.shape[dim] - width, None, axis=dim), axis, forward
        )
        high = lax.ppermute(lax.slice_in_dim(block, 0, width, axis=dim), axis, backward)
        block = jnp.concatenate([low, block, high], axis=dim)
    return block


def passed_along(value, axis, by):
    devices = lax.axis_size(axis)
    pairs = [(i, i + by) for i in range(devices) if 0 <= i + by < devices]
    return lax.ppermute(value, axis, pairs)


def extend_rows(field):
    return with_halo(field, (("rows", 1),), 1)


def with_prior(field):
    earlier = passed_along(field[-2:], "frames", 1)
    return jnp.concatenate([earlier, field], axis=0)


def with_later(field):
    following = passed_along(field[:2], "frames", -1)
    return jnp.concatenate([field, following], axis=0)


def spatial_taps(extended, row_count, col_count, flipped):
    padded = jnp.pad(extended, ((0, 0), (0, 0), (0, 0), (1, 1)))
    pieces = []
    for i in range(3):
        for j in range(3):
            row_start = 2 - i if flipped else i
            col_start = 2 - j if flipped else j
            pieces.append(
                padded[:, row_start : row_start + row_count, :, col_start : col_start + col_count]
            )
    return jnp.concatenate(pieces, axis=2)


def forward_conv(extended, kernel, frame_count, row_count, col_count):
    taps = spatial_taps(extended, row_count, col_count, False)
    chan_out = kernel.shape[3]
    running = None
    for t in range(3):
        flat_kernel = jnp.transpose(kernel[t], (2, 0, 1, 3)).reshape((chan_out, -1))
        term = jnp.einsum(
            "ok,frkw->frow",
            flat_kernel,
            taps[t : t + frame_count],
            preferred_element_type=jnp.float32,
        )
        running = term if running is None else running + term
    return running


def adjoint_conv(extended, kernel, frame_count, row_count, col_count):
    taps = spatial_taps(extended, row_count, col_count, True)
    chan_in = kernel.shape[4]
    running = None
    for t in range(3):
        flat_kernel = jnp.transpose(kernel[t], (3, 0, 1, 2)).reshape((chan_in, -1))
        term = jnp.einsum(
            "ck,frkw->frcw",
            flat_kernel,
            taps[2 - t : 2 - t + frame_count],
            preferred_element_type=jnp.float32,
        )
        running = term if running is None else running + term
    return running


def kernel_grad(upstream, extended):
    frame_count, row_count, chan_out, col_count = upstream.shape
    chan_in = extended.shape[2]
    taps = spatial_taps(extended, row_count, col_count, False)
    pieces = []
    for t in range(3):
        flat = jnp.einsum(
            "frow,frkw->ok", upstream, taps[t : t + frame_count], preferred_element_type=jnp.float32
        )
        pieces.append(jnp.transpose(flat.reshape((chan_out, 3, 3, chan_in)), (1, 2, 0, 3)))
    return jnp.stack(pieces, axis=0)


def per_device(clip_in, kernel_one, bias_one, kernel_two, cotangent):
    frame_count, row_count, channels, col_count = clip_in.shape
    input_rows = extend_rows(clip_in)
    cot_rows = None
    input_ext = with_prior(input_rows)
    hidden = (
        forward_conv(input_ext, kernel_one, frame_count, row_count, col_count)
        + bias_one[None, None, :, None]
    )
    active = jax.nn.silu(hidden).astype(jnp.bfloat16)
    active_ext = with_prior(extend_rows(active))
    block_out = (
        clip_in.astype(jnp.float32)
        + forward_conv(active_ext, kernel_two, frame_count, row_count, col_count)
    ).astype(jnp.bfloat16)
    cot_rows = extend_rows(cotangent)
    cot_ext = with_later(cot_rows)
    grad_act = adjoint_conv(cot_ext, kernel_two, frame_count, row_count, col_count)
    sig = jax.nn.sigmoid(hidden)
    grad_pre = (grad_act * sig * (1.0 + hidden * (1.0 - sig))).astype(jnp.bfloat16)
    pre_ext = with_later(extend_rows(grad_pre))
    grad_back = adjoint_conv(pre_ext, kernel_one, frame_count, row_count, col_count)
    grad_input = (cotangent.astype(jnp.float32) + grad_back).astype(jnp.bfloat16)
    term_second = kernel_grad(cotangent, active_ext)
    term_first = kernel_grad(grad_pre, input_ext)
    term_bias = jnp.sum(grad_pre.astype(jnp.float32), axis=(0, 1, 3))
    total_first, total_second, total_bias = lax.psum(
        (term_first, term_second, term_bias), ("frames", "rows")
    )
    cell_total = (
        frame_count * lax.axis_size("frames") * row_count * lax.axis_size("rows") * col_count
    )
    inv_scale = 1.0 / math.sqrt(cell_total)
    return (
        block_out,
        grad_input,
        total_first * inv_scale,
        total_second * inv_scale,
        total_bias * inv_scale,
    )


def solution(mesh):
    in_specs = (P("frames", "rows", None, None), P(), P(), P(), P("frames", "rows", None, None))
    out_specs = (P("frames", "rows", None, None), P("frames", "rows", None, None), P(), P(), P())
    return jax.shard_map(
        per_device, mesh=mesh, in_specs=in_specs, out_specs=out_specs, check_vma=False
    )
```

profile of v0, /device:TPU:0, one launch (start us, length us, event | category | flops | bytes accessed | tf_op | source)
XLA Modules:
  0.0 284.0 jit_solution(4800051043219047699)
XLA Ops:
  7.2 1.7 fusion.59
  9.0 1.3 collective-permute-start.1
  10.2 6.2 %collective-permute-start = (bf16[4,1,64,256]{3,2,1,0:T(8,128)(2,1)}, bf16[4,1,64,256]{3,2,1,0:T(8,128)(2,1)}, u32[]{:S(2)}, u32[]{:S(2)}) collective-permute-start(bf16[4,1,64,256]{3,2,1,0:T(8,128)(2,1)} %get-tuple-element.19), channel_id=1, source_target_pairs={{0,1},{1,2},{2,3},{3,4},{4,5},{5,6},{6,7},{8,9},{9,10},{10,11},{11... | collective-permute-start | bytes 393224 | tf_op jit(solution)/shard_map/ppermute | solution.py:14
  16.4 1.0 fusion.57
  17.4 1.3 collective-permute-start.7
  18.7 4.8 %collective-permute-start.6 = (bf16[4,1,64,256]{3,2,1,0:T(8,128)(2,1)S(1)}, bf16[4,1,64,256]{3,2,1,0:T(8,128)(2,1)S(1)}, u32[]{:S(2)}, u32[]{:S(2)}) collective-permute-start(bf16[4,1,64,256]{3,2,1,0:T(8,128)(2,1)S(1)} %get-tuple-element.15), channel_id=1, source_target_pairs={{0,1},{1,2},{2,3},{3,4},{4,5},{5,6},{6,7},{8,9},{9,10},{10,11},{11... | collective-permute-start | bytes 393224 | tf_op jit(solution)/shard_map/ppermute | solution.py:14
  23.5 2.0 fusion.60
  25.5 2.0 collective-permute-done.6
  27.5 1.1 constant_dynamic-update-slice_fusion.4
  28.6 1.3 collective-permute-start.8
  29.9 1.9 fusion.61
  31.9 0.8 copy.28
  33.3 0.8 copy.38
  34.1 0.9 constant_dynamic-update-slice_fusion.2
  35.1 3.1 %collective-permute-start.2 = (bf16[2,6,64,256]{3,2,1,0:T(8,128)(2,1)S(1)}, bf16[2,6,64,256]{3,2,1,0:T(8,128)(2,1)S(1)}, u32[]{:S(2)}, u32[]{:S(2)}) collective-permute-start(bf16[2,6,64,256]{3,2,1,0:T(8,128)(2,1)S(1)} %slice.306), channel_id=1, source_target_pairs={{0,8},{8,16},{16,24},{1,9},{9,17},{17,25},{2,10},{10,18},{18,26},{... | collective-permute-start | bytes 1179656 | tf_op jit(solution)/shard_map/ppermute | solution.py:25
  40.4 1.0 fusion.66
  41.5 1.0 fusion.65
  44.9 1.0 fusion.63
  46.0 1.0 fusion.62
  47.0 1.3 multiply_convert_fusion
  48.3 1.5 convert_reduce_fusion
  49.8 1.4 fusion
  51.2 2.1 fusion.2
  53.3 2.1 fusion.4
  55.4 4.4 %collective-permute-start.3 = (bf16[4,1,64,256]{3,2,1,0:T(8,128)(2,1)S(1)}, bf16[4,1,64,256]{3,2,1,0:T(8,128)(2,1)S(1)}, u32[]{:S(2)}, u32[]{:S(2)}) collective-permute-start(bf16[4,1,64,256]{3,2,1,0:T(8,128)(2,1)S(1)} %get-tuple-element.16), channel_id=1, source_target_pairs={{0,1},{1,2},{2,3},{3,4},{4,5},{5,6},{6,7},{8,9},{9,10},{10,11},{11... | collective-permute-start | bytes 393224 | tf_op jit(solution)/shard_map/ppermute | solution.py:14
  59.8 1.3 collective-permute-start.4
  61.1 4.9 %collective-permute-start.9 = (bf16[4,1,64,256]{3,2,1,0:T(8,128)(2,1)S(1)}, bf16[4,1,64,256]{3,2,1,0:T(8,128)(2,1)S(1)}, u32[]{:S(2)}, u32[]{:S(2)}) collective-permute-start(bf16[4,1,64,256]{3,2,1,0:T(8,128)(2,1)S(1)} %get-tuple-element.12), channel_id=1, source_target_pairs={{0,1},{1,2},{2,3},{3,4},{4,5},{5,6},{6,7},{8,9},{9,10},{10,11},{11... | collective-permute-start | bytes 393224 | tf_op jit(solution)/shard_map/ppermute | solution.py:14
  66.0 1.3 collective-permute-start.10
  67.3 44.9 %psum.23 = f32[64]{0:T(128)S(1)} all-reduce(f32[64]{0:T(128)S(1)} %get-tuple-element.34), channel_id=1, replica_groups=mesh['frames'=4,'rows'=8] {'frames','rows'}, use_global_device_ids=true, to_apply=%region_3.4 | all-reduce | flops 64 | bytes 512 | tf_op jit(solution)/shard_map/psum | solution.py:126
  112.3 1.3 collective-permute-start.5
  114.1 2.1 pad_maximum_fusion.3
  116.2 0.8 pad_maximum_fusion.5
  117.0 1.5 collective-permute-start.11
  120.8 1.5 convolution_bitcast_fusion
  122.4 1.5 convolution_bitcast_fusion.1
  123.9 1.5 convolution_bitcast_fusion.2
  125.8 4.4 %fusion.64 = f32[4,4,256,64]{2,3,1,0:T(8,128)} fusion(bf16[6,4,576,256]{3,2,1,0:T(8,128)(2,1)} %copy-done, bf16[64,576,1,1]{0,1,3,2:T(8,128)(2,1)S(1)} %bitcast.194), kind=kOutput, calls=%fused_computation.143 | convolution fusion | flops 301989888 | bytes 8200192 | tf_op jit(solution)/shard_map/ok,frkw->frow/dot_general | solution.py:61
  132.6 2.9 %copy-done.1 = bf16[6,4,576,256]{3,2,1,0:T(8,128)(2,1)} copy-done((bf16[6,4,576,256]{3,2,1,0:T(8,128)(2,1)}, bf16[6,4,576,256]{3,2,1,0:T(8,128)(2,1)S(1)}, u32[]{:S(2)}) %copy-start.1) | copy-done | bytes 7077912
  135.5 1.0 pad_maximum_fusion.4
  136.5 3.9 %convolution_add_fusion.4 = f32[4,4,256,64]{2,3,1,0:T(8,128)S(1)} fusion(f32[4,4,256,64]{2,3,1,0:T(8,128)} %fusion.64, bf16[6,4,576,256]{3,2,1,0:T(8,128)(2,1)} %copy-done, bf16[64,576,1,1]{0,1,3,2:T(8,128)(2,1)S(1)} %bitcast.192), kind=kOutput, calls=%fused_computation.44 | convolution fusion | flops 302252032 | bytes 9248768 | tf_op jit(solution)/shard_map/ok,frkw->frow/dot_general | solution.py:61
  140.4 4.3 %fusion.19 = bf16[4,4,64,256]{3,2,1,0:T(8,128)(2,1)} fusion(f32[4,4,256,64]{2,3,1,0:T(8,128)S(1)} %convolution_add_fusion.4, bf16[6,4,576,256]{3,2,1,0:T(8,128)(2,1)} %copy-done, bf16[64,576,1,1]{0,1,3,2:T(8,128)(2,1)} %bitcast.193, bf16[4,4,64,256]{3,2,1,0:T(8,128)(2,1)S(1)} %copy-done.4), kind=kOutput, calls=%fused_computation.63 | convolution fusion | flops 303038464 | bytes 9248768 | tf_op jit(solution)/shard_map/ok,frkw->frow/dot_general | solution.py:61
  144.8 1.1 fusion.67
  145.8 1.1 convolution_add_fusion.1
  146.9 1.9 fusion.17
  148.9 124.2 %all-reduce.7.cloned.1.call-done = (f32[3,3,3,64,64]{3,4,2,1,0:T(8,128)}, f32[3,3,3,64,64]{3,4,2,1,0:T(8,128)}) async-done(((f32[3,3,3,64,64]{3,4,2,1,0:T(8,128)}, f32[3,3,3,64,64]{3,4,2,1,0:T(8,128)}), (f32[3,3,3,64,64]{3,4,2,1,0:T(8,128)}, f32[3,3,3,64,64]{3,4,2,1,0:T(8,128)})) %all-reduce.7.cloned.1.call-update) | async-done | bytes 884752 | tf_op jit(solution)/shard_map/psum | solution.py:126
  273.1 1.6 broadcast_multiply_fusion
  274.7 1.2 copy.53
  275.9 1.2 copy.52
  (96 shorter events, 11.0 us)
Async XLA Ops:
  7.2 27.8 %copy-start.3 = (bf16[4,4,64,256]{3,2,1,0:T(8,128)(2,1)S(1)}, bf16[4,4,64,256]{3,2,1,0:T(8,128)(2,1)}, u32[]{:S(2)}) copy-start(bf16[4,4,64,256]{3,2,1,0:T(8,128)(2,1)} %param.5) | copy-start | bytes 1572868
  7.2 265.9 %all-reduce.7.cloned.1.call-start = ((), (), s32[]{:S(2)}) async-start(), calls=%async_computation | async-start | bytes 3538944 | tf_op jit(solution)/shard_map/psum | solution.py:126
  9.0 26.1 %collective-permute-start.1 = (bf16[4,1,64,256]{3,2,1,0:T(8,128)(2,1)}, bf16[4,1,64,256]{3,2,1,0:T(8,128)(2,1)S(1)}, u32[]{:S(2)}, u32[]{:S(2)}) collective-permute-start(bf16[4,1,64,256]{3,2,1,0:T(8,128)(2,1)} %get-tuple-element.18), channel_id=1, source_target_pairs={{1,0},{2,1},{3,2},{4,3},{5,4},{6,5},{7,6},{9,8},{10,9},{11,10},{12... | collective-permute-start | bytes 393224 | tf_op jit(solution)/shard_map/ppermute | solution.py:17
  10.2 23.8 %collective-permute-start = (bf16[4,1,64,256]{3,2,1,0:T(8,128)(2,1)}, bf16[4,1,64,256]{3,2,1,0:T(8,128)(2,1)}, u32[]{:S(2)}, u32[]{:S(2)}) collective-permute-start(bf16[4,1,64,256]{3,2,1,0:T(8,128)(2,1)} %get-tuple-element.19), channel_id=1, source_target_pairs={{0,1},{1,2},{2,3},{3,4},{4,5},{5,6},{6,7},{8,9},{9,10},{10,11},{11... | collective-permute-start | bytes 393224 | tf_op jit(solution)/shard_map/ppermute | solution.py:14
  17.4 11.2 %collective-permute-start.7 = (bf16[4,1,64,256]{3,2,1,0:T(8,128)(2,1)S(1)}, bf16[4,1,64,256]{3,2,1,0:T(8,128)(2,1)S(1)}, u32[]{:S(2)}, u32[]{:S(2)}) collective-permute-start(bf16[4,1,64,256]{3,2,1,0:T(8,128)(2,1)S(1)} %get-tuple-element.14), channel_id=1, source_target_pairs={{1,0},{2,1},{3,2},{4,3},{5,4},{6,5},{7,6},{9,8},{10,9},{11,10},{12... | collective-permute-start | bytes 393224 | tf_op jit(solution)/shard_map/ppermute | solution.py:17
  18.7 8.8 %collective-permute-start.6 = (bf16[4,1,64,256]{3,2,1,0:T(8,128)(2,1)S(1)}, bf16[4,1,64,256]{3,2,1,0:T(8,128)(2,1)S(1)}, u32[]{:S(2)}, u32[]{:S(2)}) collective-permute-start(bf16[4,1,64,256]{3,2,1,0:T(8,128)(2,1)S(1)} %get-tuple-element.15), channel_id=1, source_target_pairs={{0,1},{1,2},{2,3},{3,4},{4,5},{5,6},{6,7},{8,9},{9,10},{10,11},{11... | collective-permute-start | bytes 393224 | tf_op jit(solution)/shard_map/ppermute | solution.py:14
  28.6 9.5 %collective-permute-start.8 = (bf16[2,6,64,256]{3,2,1,0:T(8,128)(2,1)S(1)}, bf16[2,6,64,256]{3,2,1,0:T(8,128)(2,1)S(1)}, u32[]{:S(2)}, u32[]{:S(2)}) collective-permute-start(bf16[2,6,64,256]{3,2,1,0:T(8,128)(2,1)S(1)} %slice.318), channel_id=1, source_target_pairs={{8,0},{16,8},{24,16},{9,1},{17,9},{25,17},{10,2},{18,10},{26,18},{... | collective-permute-start | bytes 1179656 | tf_op jit(solution)/shard_map/ppermute | solution.py:25
  35.1 7.4 %collective-permute-start.2 = (bf16[2,6,64,256]{3,2,1,0:T(8,128)(2,1)S(1)}, bf16[2,6,64,256]{3,2,1,0:T(8,128)(2,1)S(1)}, u32[]{:S(2)}, u32[]{:S(2)}) collective-permute-start(bf16[2,6,64,256]{3,2,1,0:T(8,128)(2,1)S(1)} %slice.306), channel_id=1, source_target_pairs={{0,8},{8,16},{16,24},{1,9},{9,17},{17,25},{2,10},{10,18},{18,26},{... | collective-permute-start | bytes 1179656 | tf_op jit(solution)/shard_map/ppermute | solution.py:25
  44.5 2.5 copy-start.8
  44.6 2.5 copy-start.10
  46.0 2.4 copy-start.9
  55.4 56.8 %collective-permute-start.3 = (bf16[4,1,64,256]{3,2,1,0:T(8,128)(2,1)S(1)}, bf16[4,1,64,256]{3,2,1,0:T(8,128)(2,1)S(1)}, u32[]{:S(2)}, u32[]{:S(2)}) collective-permute-start(bf16[4,1,64,256]{3,2,1,0:T(8,128)(2,1)S(1)} %get-tuple-element.16), channel_id=1, source_target_pairs={{0,1},{1,2},{2,3},{3,4},{4,5},{5,6},{6,7},{8,9},{9,10},{10,11},{11... | collective-permute-start | bytes 393224 | tf_op jit(solution)/shard_map/ppermute | solution.py:14
  59.8 52.4 %collective-permute-start.4 = (bf16[4,1,64,256]{3,2,1,0:T(8,128)(2,1)S(1)}, bf16[4,1,64,256]{3,2,1,0:T(8,128)(2,1)S(1)}, u32[]{:S(2)}, u32[]{:S(2)}) collective-permute-start(bf16[4,1,64,256]{3,2,1,0:T(8,128)(2,1)S(1)} %get-tuple-element.17), channel_id=1, source_target_pairs={{1,0},{2,1},{3,2},{4,3},{5,4},{6,5},{7,6},{9,8},{10,9},{11,10},{12... | collective-permute-start | bytes 393224 | tf_op jit(solution)/shard_map/ppermute | solution.py:17
  61.1 55.0 %collective-permute-start.9 = (bf16[4,1,64,256]{3,2,1,0:T(8,128)(2,1)S(1)}, bf16[4,1,64,256]{3,2,1,0:T(8,128)(2,1)S(1)}, u32[]{:S(2)}, u32[]{:S(2)}) collective-permute-start(bf16[4,1,64,256]{3,2,1,0:T(8,128)(2,1)S(1)} %get-tuple-element.12), channel_id=1, source_target_pairs={{0,1},{1,2},{2,3},{3,4},{4,5},{5,6},{6,7},{8,9},{9,10},{10,11},{11... | collective-permute-start | bytes 393224 | tf_op jit(solution)/shard_map/ppermute | solution.py:14
  66.0 50.2 %collective-permute-start.10 = (bf16[4,1,64,256]{3,2,1,0:T(8,128)(2,1)S(1)}, bf16[4,1,64,256]{3,2,1,0:T(8,128)(2,1)S(1)}, u32[]{:S(2)}, u32[]{:S(2)}) collective-permute-start(bf16[4,1,64,256]{3,2,1,0:T(8,128)(2,1)S(1)} %get-tuple-element.13), channel_id=1, source_target_pairs={{1,0},{2,1},{3,2},{4,3},{5,4},{6,5},{7,6},{9,8},{10,9},{11,10},{12... | collective-permute-start | bytes 393224 | tf_op jit(solution)/shard_map/ppermute | solution.py:17
  112.3 6.2 %collective-permute-start.5 = (bf16[2,6,64,256]{3,2,1,0:T(8,128)(2,1)S(1)}, bf16[2,6,64,256]{3,2,1,0:T(8,128)(2,1)S(1)}, u32[]{:S(2)}, u32[]{:S(2)}) collective-permute-start(bf16[2,6,64,256]{3,2,1,0:T(8,128)(2,1)S(1)} %pad_maximum_fusion.7), channel_id=1, source_target_pairs={{0,8},{8,16},{16,24},{1,9},{9,17},{17,25},{2,10},{10,18},{18,26},{... | collective-permute-start | bytes 1179656 | tf_op jit(solution)/shard_map/ppermute | solution.py:25
  117.0 13.3 %collective-permute-start.11 = (bf16[2,6,64,256]{3,2,1,0:T(8,128)(2,1)}, bf16[2,6,64,256]{3,2,1,0:T(8,128)(2,1)S(1)}, u32[]{:S(2)}, u32[]{:S(2)}) collective-permute-start(bf16[2,6,64,256]{3,2,1,0:T(8,128)(2,1)} %pad_maximum_fusion.5), channel_id=1, source_target_pairs={{8,0},{16,8},{24,16},{9,1},{17,9},{25,17},{10,2},{18,10},{26,18},{... | collective-permute-start | bytes 1179656 | tf_op jit(solution)/shard_map/ppermute | solution.py:25
  118.9 1.9 copy-start.2
  120.8 3.0 %copy-start = (bf16[6,4,576,256]{3,2,1,0:T(8,128)(2,1)}, bf16[6,4,576,256]{3,2,1,0:T(8,128)(2,1)S(1)}, u32[]{:S(2)}) copy-start(bf16[6,4,576,256]{3,2,1,0:T(8,128)(2,1)S(1)} %fusion.43) | copy-start | bytes 21233668
  132.6 2.9 %copy-start.1 = (bf16[6,4,576,256]{3,2,1,0:T(8,128)(2,1)}, bf16[6,4,576,256]{3,2,1,0:T(8,128)(2,1)S(1)}, u32[]{:S(2)}) copy-start(bf16[6,4,576,256]{3,2,1,0:T(8,128)(2,1)S(1)} %fusion.55) | copy-start | bytes 21233668
  136.5 8.3 %slice-start = ((s8[7077888]{0:T(1024)(128)(4,1)}), s8[2883584]{0:T(1024)(128)(4,1)S(1)}, s32[]{:S(2)}) async-start(s8[7077888]{0:T(1024)(128)(4,1)} %bitcast.187), calls=%async_computation.1 | async-start | bytes 5767168
  136.5 3.9 %copy-start.4 = (bf16[4,4,64,256]{3,2,1,0:T(8,128)(2,1)S(1)}, bf16[4,4,64,256]{3,2,1,0:T(8,128)(2,1)}, u32[]{:S(2)}) copy-start(bf16[4,4,64,256]{3,2,1,0:T(8,128)(2,1)} %param.5) | copy-start | bytes 1572868
  136.5 8.2 %copy-start.7 = (bf16[1,3,3,64,64]{4,3,2,1,0:T(8,128)(2,1)S(1)}, bf16[1,3,3,64,64]{4,3,2,1,0:T(8,128)(2,1)}, u32[]{:S(2)}) copy-start(bf16[1,3,3,64,64]{4,3,2,1,0:T(8,128)(2,1)} %get-tuple-element.25) | copy-start | bytes 221188
  136.5 8.2 %slice-start.1 = ((s8[7077888]{0:T(1024)(128)(4,1)}), s8[4194304]{0:T(1024)(128)(4,1)S(1)}, s32[]{:S(2)}) async-start(s8[7077888]{0:T(1024)(128)(4,1)} %bitcast.187), calls=%async_computation.2 | async-start | bytes 8388608
  140.4 5.4 %copy-start.6 = (bf16[1,3,3,64,64]{4,3,2,1,0:T(8,128)(2,1)S(1)}, bf16[1,3,3,64,64]{4,3,2,1,0:T(8,128)(2,1)}, u32[]{:S(2)}) copy-start(bf16[1,3,3,64,64]{4,3,2,1,0:T(8,128)(2,1)} %get-tuple-element.24) | copy-start | bytes 221188
  144.8 2.2 copy-start.5
Sparse Core Ops, SparseCore 0:
  136.6 136.4 all-reduce.6
where the time goes:
time: 285 us; the launch traced here: 284 us
  waiting for transfers between devices  126 us (44%)
  blocking collectives  44.9 us (16%)
  matrix products  33.6 us (12%)
  starting transfers between devices  32.5 us (11%)
  local copies, waits for them, and re-layouts  25 us (9%)
  between operations  14.8 us (5%)
  other arithmetic  6.87 us (2%)
    psum x1, waiting for transfers between devices, per_device(): lax.psum((term_first, term_second, term_bias), ('frames', 'rows'))  124 us
    psum x1, blocking collectives, per_device(): lax.psum((term_first, term_second, term_bias), ('frames', 'rows'))  44.9 us
    ppermute x4, starting transfers between devices, with_halo(): lax.ppermute(lax.slice_in_dim(block, block.shape[dim] - width, None, axis...  20.2 us
    dot_general x6, matrix products, forward_conv(): jnp.einsum('ok,frkw->frow', flat_kernel, taps[t:t + frame_count], preferr...  15.9 us
    unnamed x58, local copies, waits for them, and re-layouts  14.3 us
    dot_general x6, matrix products, kernel_grad(): jnp.einsum('frow,frkw->ok', upstream, taps[t:t + frame_count], preferred_...  10 us
    dot_general x6, matrix products, adjoint_conv(): jnp.einsum('ck,frkw->frcw', flat_kernel, taps[2 - t:2 - t + frame_count],...  7.64 us
    ppermute x4, starting transfers between devices, passed_along(): return lax.ppermute(value, axis, pairs)  7.12 us
  transfers between devices with their start and end apart: 13, of which 2 were waited for; matrix products, arithmetic and copies ran while one was open for 14% of the time, Pallas kernels for 0%

commit v1 on v0

--- a/solution.py
+++ b/solution.py
@@ -1,8 +1,11 @@
+import functools
 import math
 
 import jax
 import jax.numpy as jnp
 from jax import lax
+from jax.experimental import pallas as pl
+from jax.experimental.pallas import tpu as pltpu
 from jax.sharding import PartitionSpec as P
 
 
@@ -95,6 +98,122 @@
         )
         pieces.append(jnp.transpose(flat.reshape((chan_out, 3, 3, chan_in)), (1, 2, 0, 3)))
     return jnp.stack(pieces, axis=0)
+
+
+MESH = pl.DeviceIdType.MESH
+
+
+def remote(src, dst, send_sem, recv_sem, device):
+    return pltpu.make_async_remote_copy(
+        src_ref=src,
+        dst_ref=dst,
+        send_sem=send_sem,
+        recv_sem=recv_sem,
+        device_id=device,
+        device_id_type=MESH,
+    )
+
+
+def reduce_kernel(
+    frames, rows, g_ref, out_ref, send, got_f, part, total, got_r, full,
+    s_f, r_f, s_r, r_r, s_gr, r_gr, s_gf, r_gf,
+):
+    f, r = lax.axis_index("frames"), lax.axis_index("rows")
+    chunk_f = g_ref.shape[0] // frames
+    chunk_r = chunk_f // rows
+    barrier = pltpu.get_barrier_semaphore()
+    for d in range(1, frames):
+        pl.semaphore_signal(
+            barrier, inc=1, device_id=(lax.rem(f + d, frames), r), device_id_type=MESH
+        )
+    for d in range(1, rows):
+        pl.semaphore_signal(
+            barrier, inc=1, device_id=(f, lax.rem(r + d, rows)), device_id_type=MESH
+        )
+    pl.semaphore_wait(barrier, frames + rows - 2)
+
+    send[...] = g_ref[...].astype(jnp.bfloat16)
+    copies = []
+    for d in range(1, frames):
+        p = lax.rem(f + d, frames)
+        at = pl.multiple_of(p * chunk_f, chunk_f)
+        copies.append(
+            remote(send.at[pl.ds(at, chunk_f)], got_f.at[d - 1], s_f.at[d - 1], r_f.at[d - 1], (p, r))
+        )
+        copies[-1].start()
+    own_f = pl.multiple_of(f * chunk_f, chunk_f)
+    total[...] = g_ref[pl.ds(own_f, chunk_f)]
+    for d in range(1, frames):
+        copies[d - 1].wait_recv()
+        total[...] += got_f[d - 1].astype(jnp.float32)
+    part[...] = total[...].astype(jnp.bfloat16)
+    for d in range(1, rows):
+        q = lax.rem(r + d, rows)
+        at = pl.multiple_of(q * chunk_r, chunk_r)
+        copies.append(
+            remote(part.at[pl.ds(at, chunk_r)], got_r.at[d - 1], s_r.at[d - 1], r_r.at[d - 1], (f, q))
+        )
+        copies[-1].start()
+    mine = total[pl.ds(pl.multiple_of(r * chunk_r, chunk_r), chunk_r)]
+    for d in range(1, rows):
+        copies[frames - 2 + d].wait_recv()
+        mine = mine + got_r[d - 1].astype(jnp.float32)
+    here = pl.ds(pl.multiple_of(f * chunk_f + r * chunk_r, chunk_r), chunk_r)
+    full[here] = mine.astype(jnp.bfloat16)
+    gathers = []
+    for d in range(1, rows):
+        gathers.append(
+            remote(
+                full.at[here], full.at[here], s_gr.at[d - 1], r_gr.at[d - 1],
+                (f, lax.rem(r + d, rows)),
+            )
+        )
+        gathers[-1].start()
+    for copy in gathers:
+        copy.wait_recv()
+    block = pl.ds(own_f, chunk_f)
+    for d in range(1, frames):
+        gathers.append(
+            remote(
+                full.at[block], full.at[block], s_gf.at[d - 1], r_gf.at[d - 1],
+                (lax.rem(f + d, frames), r),
+            )
+        )
+        gathers[-1].start()
+    for copy in gathers[rows - 1 :]:
+        copy.wait_recv()
+    out_ref[...] = full[...].astype(jnp.float32)
+    for copy in copies + gathers:
+        copy.wait_send()
+
+
+def reduce_all(packed):
+    frames, rows = lax.axis_size("frames"), lax.axis_size("rows")
+    count = packed.shape[0]
+    chunk_f = count // frames
+    chunk_r = chunk_f // rows
+    dma = pltpu.SemaphoreType.DMA
+    return pl.pallas_call(
+        functools.partial(reduce_kernel, frames, rows),
+        out_shape=jax.ShapeDtypeStruct(packed.shape, jnp.float32),
+        in_specs=[pl.BlockSpec(memory_space=pltpu.VMEM)],
+        out_specs=pl.BlockSpec(memory_space=pltpu.VMEM),
+        scratch_shapes=[
+            pltpu.VMEM((count, 128), jnp.bfloat16),
+            pltpu.VMEM((frames - 1, chunk_f, 128), jnp.bfloat16),
+            pltpu.VMEM((chunk_f, 128), jnp.bfloat16),
+            pltpu.VMEM((chunk_f, 128), jnp.float32),
+            pltpu.VMEM((rows - 1, chunk_r, 128), jnp.bfloat16),
+            pltpu.VMEM((count, 128), jnp.bfloat16),
+            dma((frames - 1,)), dma((frames - 1,)),
+            dma((rows - 1,)), dma((rows - 1,)),
+            dma((rows - 1,)), dma((rows - 1,)),
+            dma((frames - 1,)), dma((frames - 1,)),
+        ],
+        compiler_params=pltpu.CompilerParams(
+            collective_id=0, has_side_effects=True, vmem_limit_bytes=32 * 1024 * 1024
+        ),
+    )(packed)
 
 
 def per_device(clip_in, kernel_one, bias_one, kernel_two, cotangent):
@@ -123,9 +242,14 @@
     term_second = kernel_grad(cotangent, active_ext)
     term_first = kernel_grad(grad_pre, input_ext)
     term_bias = jnp.sum(grad_pre.astype(jnp.float32), axis=(0, 1, 3))
-    total_first, total_second, total_bias = lax.psum(
-        (term_first, term_second, term_bias), ("frames", "rows")
-    )
+    size = term_first.size
+    step = lax.axis_size("frames") * lax.axis_size("rows") * 16 * 128
+    flat = jnp.concatenate([term_first.reshape(-1), term_second.reshape(-1), term_bias])
+    flat = jnp.pad(flat, (0, -flat.size % step))
+    total = reduce_all(flat.reshape((-1, 128))).reshape(-1)
+    total_first = total[:size].reshape(term_first.shape)
+    total_second = total[size : 2 * size].reshape(term_second.shape)
+    total_bias = total[2 * size : 2 * size + channels]
     cell_total = (
         frame_count * lax.axis_size("frames") * row_count * lax.axis_size("rows") * col_count
     )

time: 285 us -> 131 us (0.46)
  waiting for transfers between devices: 126 us -> 9.8 us
  blocking collectives: 44.9 us -> 0 us
  Pallas kernels: 0 us -> 27.7 us
  between operations: 14.8 us -> 1.47 us
  matrix products: 33.6 us -> 23.6 us
    psum x1 -> x0, waiting for transfers between devices: 124 us -> none  [per_device(): lax.psum((term_first, term_second, term_bias), ('frames', 'rows'))]
    psum x1 -> x0, blocking collectives: 44.9 us -> none  [per_device(): lax.psum((term_first, term_second, term_bias), ('frames', 'rows'))]
    pallas_call x0 -> x1, Pallas kernels: none -> 27.7 us  [reduce_all(): pl.pallas_call(functools.partial(reduce_kernel, frames, rows), out_shape=...]
    dot_general x6, matrix products: 15.9 us -> 7.39 us  [forward_conv(): jnp.einsum('ok,frkw->frow', flat_kernel, taps[t:t + frame_count], preferr...]
    ppermute x4, waiting for transfers between devices: 0.01 us -> 5.07 us  [with_halo(): lax.ppermute(lax.slice_in_dim(block, 0, width, axis=dim), axis, backward)]
    unnamed x58 -> x62, local copies, waits for them, and re-layouts: 14.3 us -> 10 us
    another operation x2, other arithmetic: 3.04 us -> 0.17 us  [kernel_grad(): return jnp.stack(pieces, axis=0)]
  transfers between devices with their start and end apart: 13 -> 12, of which waited for: 2 -> 3; matrix products, arithmetic and copies ran while one was open for 14% -> 25% of each run, Pallas kernels for 0% -> 21%
where the time goes in v1:
time: 131 us
  starting transfers between devices  34.6 us (26%)
  Pallas kernels  27.7 us (21%)
  local copies, waits for them, and re-layouts  26.1 us (20%)
  matrix products  23.6 us (18%)
  waiting for transfers between devices  9.8 us (7%)
  other arithmetic  7.42 us (6%)
  between operations  1.47 us (1%)
    pallas_call x1, Pallas kernels, reduce_all(): pl.pallas_call(functools.partial(reduce_kernel, frames, rows), out_shape=...  27.7 us
    ppermute x4, starting transfers between devices, with_halo(): lax.ppermute(lax.slice_in_dim(block, block.shape[dim] - width, None, axis...  20.9 us
    unnamed x62, local copies, waits for them, and re-layouts  10 us
    ppermute x4, starting transfers between devices, passed_along(): return lax.ppermute(value, axis, pairs)  8.62 us
    dot_general x6, matrix products, kernel_grad(): jnp.einsum('frow,frkw->ok', upstream, taps[t:t + frame_count], preferred_...  8.59 us
    dot_general x6, matrix products, adjoint_conv(): jnp.einsum('ck,frkw->frcw', flat_kernel, taps[2 - t:2 - t + frame_count],...  7.62 us
    dot_general x6, matrix products, forward_conv(): jnp.einsum('ok,frkw->frow', flat_kernel, taps[t:t + frame_count], preferr...  7.39 us
    ppermute x4, starting transfers between devices, with_halo(): lax.ppermute(lax.slice_in_dim(block, 0, width, axis=dim), axis, backward)  5.14 us
  transfers between devices with their start and end apart: 12, of which 3 were waited for; matrix products, arithmetic and copies ran while one was open for 25% of the time, Pallas kernels for 21%

profile of v1, /device:TPU:0, one launch (start us, length us, event | category | flops | bytes accessed | tf_op | source)
XLA Modules:
  0.0 130.7 jit_solution(14281336677800176067)
XLA Ops:
  0.6 1.0 fusion.58
  1.7 4.9 %collective-permute-start.6 = (bf16[4,1,64,256]{3,2,1,0:T(8,128)(2,1)S(1)}, bf16[4,1,64,256]{3,2,1,0:T(8,128)(2,1)S(1)}, u32[]{:S(2)}, u32[]{:S(2)}) collective-permute-start(bf16[4,1,64,256]{3,2,1,0:T(8,128)(2,1)S(1)} %get-tuple-element.10), channel_id=1, source_target_pairs={{0,1},{1,2},{2,3},{3,4},{4,5},{5,6},{6,7},{8,9},{9,10},{10,11},{11... | collective-permute-start | bytes 393224 | tf_op jit(solution)/shard_map/ppermute | solution.py:17
  6.6 1.3 collective-permute-start.7
  7.9 1.7 %fusion.60 = (bf16[4,1,64,256]{3,2,1,0:T(8,128)(2,1)}, bf16[4,1,64,256]{3,2,1,0:T(8,128)(2,1)}) fusion(bf16[4,4,64,256]{3,2,1,0:T(8,128)(2,1)} %param.5), kind=kLoop, calls=%fused_computation.142 | loop fusion | bytes 524288 | tf_op jit(solution)/shard_map/slice | solution.py:20
  9.6 5.2 %collective-permute-start = (bf16[4,1,64,256]{3,2,1,0:T(8,128)(2,1)}, bf16[4,1,64,256]{3,2,1,0:T(8,128)(2,1)}, u32[]{:S(2)}, u32[]{:S(2)}) collective-permute-start(bf16[4,1,64,256]{3,2,1,0:T(8,128)(2,1)} %get-tuple-element.14), channel_id=1, source_target_pairs={{0,1},{1,2},{2,3},{3,4},{4,5},{5,6},{6,7},{8,9},{9,10},{10,11},{11... | collective-permute-start | bytes 393224 | tf_op jit(solution)/shard_map/ppermute | solution.py:17
  14.8 1.3 collective-permute-start.1
  16.0 1.9 %fusion.62 = (bf16[1,3,3,64,64]{4,3,2,1,0:T(8,128)(2,1)}, bf16[64,3,3,64]{3,0,2,1:T(8,128)(2,1)S(1)}, bf16[64,3,3,64]{3,0,2,1:T(8,128)(2,1)S(1)}, bf16[64,3,3,64...) fusion(bf16[3,3,3,64,64]{4,3,2,1,0:T(8,128)(2,1)} %param.8), kind=kLoop, calls=%fused_computation.144 | loop fusion | bytes 663552 | tf_op jit(solution)/shard_map/slice | solution.py:63
  18.0 1.1 constant_dynamic-update-slice_fusion.4
  19.1 1.3 collective-permute-start.8
  20.4 2.0 %fusion.61 = (bf16[1,3,3,64,64]{4,3,2,1,0:T(8,128)(2,1)}, bf16[64,3,3,64]{3,0,2,1:T(8,128)(2,1)S(1)}, bf16[64,3,3,64]{3,0,2,1:T(8,128)(2,1)S(1)}, bf16[64,3,3,64...) fusion(bf16[3,3,3,64,64]{4,3,2,1,0:T(8,128)(2,1)} %param.6), kind=kLoop, calls=%fused_computation.143 | loop fusion | bytes 663552 | tf_op jit(solution)/shard_map/slice | solution.py:63
  25.3 0.9 constant_dynamic-update-slice_fusion.2
  26.3 3.1 %collective-permute-start.2 = (bf16[2,6,64,256]{3,2,1,0:T(8,128)(2,1)S(1)}, bf16[2,6,64,256]{3,2,1,0:T(8,128)(2,1)S(1)}, u32[]{:S(2)}, u32[]{:S(2)}) collective-permute-start(bf16[2,6,64,256]{3,2,1,0:T(8,128)(2,1)S(1)} %slice.320), channel_id=1, source_target_pairs={{0,8},{8,16},{16,24},{1,9},{9,17},{17,25},{2,10},{10,18},{18,26},{... | collective-permute-start | bytes 1179656 | tf_op jit(solution)/shard_map/ppermute | solution.py:28
  31.6 1.0 fusion.66
  32.7 1.0 fusion.67
  36.1 1.0 fusion.63
  37.2 1.0 fusion.64
  38.2 1.3 multiply_convert_fusion
  39.5 1.5 %convert_reduce_fusion = (f32[64]{0:T(128)S(1)}, bf16[4,4,64,256]{3,2,1,0:T(8,128)(2,1)S(1)}) fusion(f32[4,4,64,256]{3,2,1,0:T(8,128)S(1)} %get-tuple-element.28, f32[4,4,256,64]{2,3,1,0:T(8,128)S(1)} %fusion.67, f32[4,4,256,64]{2,3,1,0:T(8,128)S(1)} %fusion.66, bf16[6,4,576,256]{3,2,1,0:T(8,128)(2,1)S(1)} %fusion.50, bf16[64,576,1,1]{0,1,3,2:T(8,128)(2,1)S(1)} %bitcast.214), kind=kOutput, calls=%fused_computation.73 | convolution fusion | flops 305397696 | bytes 10821888 | tf_op jit(solution)/shard_map/ck,frkw->frcw/dot_general | solution.py:80
  41.0 1.4 %fusion.4 = f32[64,576,1,1]{0,1,3,2:T(8,128)S(1)} fusion(bf16[4,4,64,256]{3,2,1,0:T(8,128)(2,1)S(1)} %get-tuple-element.30, bf16[6,4,576,256]{3,2,1,0:T(8,128)(2,1)S(1)} %fusion.38), kind=kOutput, calls=%fused_computation.4 | convolution fusion | flops 301989888 | bytes 5390336 | tf_op jit(solution)/shard_map/frow,frkw->ok/dot_general | solution.py:96
  42.4 1.4 %fusion.2 = f32[64,576,1,1]{0,1,3,2:T(8,128)S(1)} fusion(bf16[4,4,64,256]{3,2,1,0:T(8,128)(2,1)S(1)} %get-tuple-element.30, bf16[6,4,576,256]{3,2,1,0:T(8,128)(2,1)S(1)} %fusion.38), kind=kOutput, calls=%fused_computation.2 | convolution fusion | flops 301989888 | bytes 5390336 | tf_op jit(solution)/shard_map/frow,frkw->ok/dot_general | solution.py:96
  43.8 4.5 %collective-permute-start.3 = (bf16[4,1,64,256]{3,2,1,0:T(8,128)(2,1)S(1)}, bf16[4,1,64,256]{3,2,1,0:T(8,128)(2,1)S(1)}, u32[]{:S(2)}, u32[]{:S(2)}) collective-permute-start(bf16[4,1,64,256]{3,2,1,0:T(8,128)(2,1)S(1)} %get-tuple-element.11), channel_id=1, source_target_pairs={{0,1},{1,2},{2,3},{3,4},{4,5},{5,6},{6,7},{8,9},{9,10},{10,11},{11... | collective-permute-start | bytes 393224 | tf_op jit(solution)/shard_map/ppermute | solution.py:17
  48.4 1.3 collective-permute-start.4
  49.7 1.4 %fusion = f32[64,576,1,1]{0,1,3,2:T(8,128)S(1)} fusion(bf16[4,4,64,256]{3,2,1,0:T(8,128)(2,1)S(1)} %get-tuple-element.30, bf16[6,4,576,256]{3,2,1,0:T(8,128)(2,1)S(1)} %fusion.38), kind=kOutput, calls=%fused_computation | convolution fusion | flops 301989888 | bytes 5390336 | tf_op jit(solution)/shard_map/frow,frkw->ok/dot_general | solution.py:96
  51.0 0.8 collective-permute-done.3
  51.9 5.1 %collective-permute-done.4 = bf16[4,1,64,256]{3,2,1,0:T(8,128)(2,1)S(1)} collective-permute-done((bf16[4,1,64,256]{3,2,1,0:T(8,128)(2,1)S(1)}, bf16[4,1,64,256]{3,2,1,0:T(8,128)(2,1)S(1)}, u32[]{:S(2)}, u32[]{:S(2)}) %collective-permute-start.4) | collective-permute-done | bytes 131104 | tf_op jit(solution)/shard_map/ppermute | solution.py:20
  57.7 2.8 %collective-permute-start.5 = (bf16[2,6,64,256]{3,2,1,0:T(8,128)(2,1)}, bf16[2,6,64,256]{3,2,1,0:T(8,128)(2,1)}, u32[]{:S(2)}, u32[]{:S(2)}) collective-permute-start(bf16[2,6,64,256]{3,2,1,0:T(8,128)(2,1)} %pad_maximum_fusion.7), channel_id=1, source_target_pairs={{0,8},{8,16},{16,24},{1,9},{9,17},{17,25},{2,10},{10,18},{18,26},{... | collective-permute-start | bytes 1179656 | tf_op jit(solution)/shard_map/ppermute | solution.py:28
  61.3 1.3 collective-permute-start.10
  62.6 6.3 %collective-permute-start.9 = (bf16[4,1,64,256]{3,2,1,0:T(8,128)(2,1)}, bf16[4,1,64,256]{3,2,1,0:T(8,128)(2,1)}, u32[]{:S(2)}, u32[]{:S(2)}) collective-permute-start(bf16[4,1,64,256]{3,2,1,0:T(8,128)(2,1)} %get-tuple-element.7), channel_id=1, source_target_pairs={{0,1},{1,2},{2,3},{3,4},{4,5},{5,6},{6,7},{8,9},{9,10},{10,11},{11... | collective-permute-start | bytes 393224 | tf_op jit(solution)/shard_map/ppermute | solution.py:17
  69.2 1.0 reshape.102
  70.2 3.9 %collective-permute-done.9 = bf16[4,1,64,256]{3,2,1,0:T(8,128)(2,1)} collective-permute-done((bf16[4,1,64,256]{3,2,1,0:T(8,128)(2,1)}, bf16[4,1,64,256]{3,2,1,0:T(8,128)(2,1)}, u32[]{:S(2)}, u32[]{:S(2)}) %collective-permute-start.9) | collective-permute-done | bytes 131104 | tf_op jit(solution)/shard_map/ppermute | solution.py:17
  74.1 1.7 %pad_maximum_fusion.5 = bf16[2,6,64,256]{3,2,1,0:T(8,128)(2,1)} fusion(bf16[4,1,64,256]{3,2,1,0:T(8,128)(2,1)S(1)} %collective-permute-done.10, bf16[4,4,64,256]{3,2,1,0:T(8,128)(2,1)S(1)} %get-tuple-element.30, bf16[4,1,64,256]{3,2,1,0:T(8,128)(2,1)} %collective-permute-done.9), kind=kLoop, calls=%fused_computation.122 | loop fusion | flops 393216 | bytes 1179648 | tf_op jit(solution)/shard_map/concatenate | solution.py:21
  75.7 1.5 %collective-permute-start.11 = (bf16[2,6,64,256]{3,2,1,0:T(8,128)(2,1)}, bf16[2,6,64,256]{3,2,1,0:T(8,128)(2,1)}, u32[]{:S(2)}, u32[]{:S(2)}) collective-permute-start(bf16[2,6,64,256]{3,2,1,0:T(8,128)(2,1)} %pad_maximum_fusion.5), channel_id=1, source_target_pairs={{8,0},{16,8},{24,16},{9,1},{17,9},{25,17},{10,2},{18,10},{26,18},{... | collective-permute-start | bytes 1179656 | tf_op jit(solution)/shard_map/ppermute | solution.py:28
  77.2 1.3 maximum_maximum_fusion
  80.8 1.5 %convolution_bitcast_fusion.2 = f32[64,576]{1,0:T(8,128)S(1)} fusion(bf16[6,4,576,256]{3,2,1,0:T(8,128)(2,1)S(1)} %fusion.44, bf16[4,4,64,256]{3,2,1,0:T(8,128)(2,1)S(1)} %copy-done.1), kind=kOutput, calls=%fused_computation.68 | convolution fusion | flops 301989888 | bytes 7749632 | tf_op jit(solution)/shard_map/frow,frkw->ok/dot_general | solution.py:96
  82.3 1.5 %convolution_bitcast_fusion.1 = f32[64,576]{1,0:T(8,128)S(1)} fusion(bf16[6,4,576,256]{3,2,1,0:T(8,128)(2,1)S(1)} %fusion.44, bf16[4,4,64,256]{3,2,1,0:T(8,128)(2,1)S(1)} %copy-done.1), kind=kOutput, calls=%fused_computation.67 | convolution fusion | flops 301989888 | bytes 7749632 | tf_op jit(solution)/shard_map/frow,frkw->ok/dot_general | solution.py:96
  83.8 1.5 %convolution_bitcast_fusion = f32[64,576]{1,0:T(8,128)S(1)} fusion(bf16[6,4,576,256]{3,2,1,0:T(8,128)(2,1)S(1)} %fusion.44, bf16[4,4,64,256]{3,2,1,0:T(8,128)(2,1)S(1)} %copy-done.1), kind=kOutput, calls=%fused_computation.66 | convolution fusion | flops 301989888 | bytes 7749632 | tf_op jit(solution)/shard_map/frow,frkw->ok/dot_general | solution.py:96
  86.3 1.1 fusion.20.g_ref
  87.4 27.7 %shard_map.92 = f32[2048,128]{1,0:T(8,128)S(1)} custom-call(f32[2048,128]{1,0:T(8,128)S(1)} %fusion.20.g_ref), custom_call_target="tpu_custom_call" | custom-call | tf_op jit(solution)/shard_map/pallas_call | solution.py:196
  115.2 1.1 mul.36
  116.3 1.1 mul.38
  118.0 1.2 pad_maximum_fusion.2
  121.5 1.1 slice-done.1
  122.6 1.0 fusion.65
  123.7 1.0 fusion.68
  124.7 1.1 convolution_add_fusion.1
  125.8 1.9 %fusion.17 = bf16[4,4,64,256]{3,2,1,0:T(8,128)(2,1)} fusion(f32[4,4,256,64]{2,3,1,0:T(8,128)S(1)} %convolution_add_fusion.1, bf16[6,4,576,256]{3,2,1,0:T(8,128)(2,1)S(1)} %fusion.56, bf16[64,576,1,1]{0,1,3,2:T(8,128)(2,1)S(1)} %bitcast.205, bf16[4,4,64,256]{3,2,1,0:T(8,128)(2,1)S(1)} %copy-done.1), kind=kOutput, calls=%fused_computation.61 | convolution fusion | flops 303038464 | bytes 9248768 | tf_op jit(solution)/shard_map/ck,frkw->frcw/dot_general | solution.py:80
  127.7 1.0 convolution_add_fusion.4
  128.8 1.9 %fusion.19 = bf16[4,4,64,256]{3,2,1,0:T(8,128)(2,1)} fusion(f32[4,4,256,64]{2,3,1,0:T(8,128)S(1)} %convolution_add_fusion.4, bf16[6,4,576,256]{3,2,1,0:T(8,128)(2,1)S(1)} %bitcast.196, bf16[64,576,1,1]{0,1,3,2:T(8,128)(2,1)S(1)} %bitcast.200, bf16[4,4,64,256]{3,2,1,0:T(8,128)(2,1)S(1)} %copy-done.2), kind=kOutput, calls=%fused_computation.63 | convolution fusion | flops 303038464 | bytes 9248768 | tf_op jit(solution)/shard_map/ok,frkw->frow/dot_general | solution.py:64
  (104 shorter events, 15.3 us)
Async XLA Ops:
  0.6 25.6 %copy-start.2 = (bf16[4,4,64,256]{3,2,1,0:T(8,128)(2,1)S(1)}, bf16[4,4,64,256]{3,2,1,0:T(8,128)(2,1)}, u32[]{:S(2)}) copy-start(bf16[4,4,64,256]{3,2,1,0:T(8,128)(2,1)} %param.5) | copy-start | bytes 1572868
  1.7 16.3 %collective-permute-start.6 = (bf16[4,1,64,256]{3,2,1,0:T(8,128)(2,1)S(1)}, bf16[4,1,64,256]{3,2,1,0:T(8,128)(2,1)S(1)}, u32[]{:S(2)}, u32[]{:S(2)}) collective-permute-start(bf16[4,1,64,256]{3,2,1,0:T(8,128)(2,1)S(1)} %get-tuple-element.10), channel_id=1, source_target_pairs={{0,1},{1,2},{2,3},{3,4},{4,5},{5,6},{6,7},{8,9},{9,10},{10,11},{11... | collective-permute-start | bytes 393224 | tf_op jit(solution)/shard_map/ppermute | solution.py:17
  6.6 12.5 %collective-permute-start.7 = (bf16[4,1,64,256]{3,2,1,0:T(8,128)(2,1)S(1)}, bf16[4,1,64,256]{3,2,1,0:T(8,128)(2,1)S(1)}, u32[]{:S(2)}, u32[]{:S(2)}) collective-permute-start(bf16[4,1,64,256]{3,2,1,0:T(8,128)(2,1)S(1)} %get-tuple-element.9), channel_id=1, source_target_pairs={{1,0},{2,1},{3,2},{4,3},{5,4},{6,5},{7,6},{9,8},{10,9},{11,10},{12... | collective-permute-start | bytes 393224 | tf_op jit(solution)/shard_map/ppermute | solution.py:20
  9.6 15.7 %collective-permute-start = (bf16[4,1,64,256]{3,2,1,0:T(8,128)(2,1)}, bf16[4,1,64,256]{3,2,1,0:T(8,128)(2,1)}, u32[]{:S(2)}, u32[]{:S(2)}) collective-permute-start(bf16[4,1,64,256]{3,2,1,0:T(8,128)(2,1)} %get-tuple-element.14), channel_id=1, source_target_pairs={{0,1},{1,2},{2,3},{3,4},{4,5},{5,6},{6,7},{8,9},{9,10},{10,11},{11... | collective-permute-start | bytes 393224 | tf_op jit(solution)/shard_map/ppermute | solution.py:17
  14.8 11.5 %collective-permute-start.1 = (bf16[4,1,64,256]{3,2,1,0:T(8,128)(2,1)}, bf16[4,1,64,256]{3,2,1,0:T(8,128)(2,1)S(1)}, u32[]{:S(2)}, u32[]{:S(2)}) collective-permute-start(bf16[4,1,64,256]{3,2,1,0:T(8,128)(2,1)} %get-tuple-element.13), channel_id=1, source_target_pairs={{1,0},{2,1},{3,2},{4,3},{5,4},{6,5},{7,6},{9,8},{10,9},{11,10},{12... | collective-permute-start | bytes 393224 | tf_op jit(solution)/shard_map/ppermute | solution.py:20
  19.1 10.2 %collective-permute-start.8 = (bf16[2,6,64,256]{3,2,1,0:T(8,128)(2,1)S(1)}, bf16[2,6,64,256]{3,2,1,0:T(8,128)(2,1)S(1)}, u32[]{:S(2)}, u32[]{:S(2)}) collective-permute-start(bf16[2,6,64,256]{3,2,1,0:T(8,128)(2,1)S(1)} %slice.332), channel_id=1, source_target_pairs={{8,0},{16,8},{24,16},{9,1},{17,9},{25,17},{10,2},{18,10},{26,18},{... | collective-permute-start | bytes 1179656 | tf_op jit(solution)/shard_map/ppermute | solution.py:28
  26.3 7.4 %collective-permute-start.2 = (bf16[2,6,64,256]{3,2,1,0:T(8,128)(2,1)S(1)}, bf16[2,6,64,256]{3,2,1,0:T(8,128)(2,1)S(1)}, u32[]{:S(2)}, u32[]{:S(2)}) collective-permute-start(bf16[2,6,64,256]{3,2,1,0:T(8,128)(2,1)S(1)} %slice.320), channel_id=1, source_target_pairs={{0,8},{8,16},{16,24},{1,9},{9,17},{17,25},{2,10},{10,18},{18,26},{... | collective-permute-start | bytes 1179656 | tf_op jit(solution)/shard_map/ppermute | solution.py:28
  35.7 2.5 %copy-start.13 = (f32[64]{0:T(128)S(1)}, f32[64]{0:T(128)}, u32[]{:S(2)}) copy-start(f32[64]{0:T(128)} %param.7) | copy-start | bytes 772
  37.1 2.4 %copy-start.12 = (bf16[1,3,3,64,64]{4,3,2,1,0:T(8,128)(2,1)S(1)}, bf16[1,3,3,64,64]{4,3,2,1,0:T(8,128)(2,1)}, u32[]{:S(2)}) copy-start(bf16[1,3,3,64,64]{4,3,2,1,0:T(8,128)(2,1)} %get-tuple-element.21) | copy-start | bytes 221188
  43.8 8.1 %collective-permute-start.3 = (bf16[4,1,64,256]{3,2,1,0:T(8,128)(2,1)S(1)}, bf16[4,1,64,256]{3,2,1,0:T(8,128)(2,1)S(1)}, u32[]{:S(2)}, u32[]{:S(2)}) collective-permute-start(bf16[4,1,64,256]{3,2,1,0:T(8,128)(2,1)S(1)} %get-tuple-element.11), channel_id=1, source_target_pairs={{0,1},{1,2},{2,3},{3,4},{4,5},{5,6},{6,7},{8,9},{9,10},{10,11},{11... | collective-permute-start | bytes 393224 | tf_op jit(solution)/shard_map/ppermute | solution.py:17
  48.4 8.6 %collective-permute-start.4 = (bf16[4,1,64,256]{3,2,1,0:T(8,128)(2,1)S(1)}, bf16[4,1,64,256]{3,2,1,0:T(8,128)(2,1)S(1)}, u32[]{:S(2)}, u32[]{:S(2)}) collective-permute-start(bf16[4,1,64,256]{3,2,1,0:T(8,128)(2,1)S(1)} %get-tuple-element.12), channel_id=1, source_target_pairs={{1,0},{2,1},{3,2},{4,3},{5,4},{6,5},{7,6},{9,8},{10,9},{11,10},{12... | collective-permute-start | bytes 393224 | tf_op jit(solution)/shard_map/ppermute | solution.py:20
  51.9 17.0 %copy-start.10 = (bf16[4,1,64,256]{3,2,1,0:T(8,128)(2,1)}, bf16[4,1,64,256]{3,2,1,0:T(8,128)(2,1)S(1)}, u32[]{:S(2)}) copy-start(bf16[4,1,64,256]{3,2,1,0:T(8,128)(2,1)S(1)} %collective-permute-done.3) | copy-start | bytes 393220
  56.9 11.9 %copy-start.11 = (bf16[4,1,64,256]{3,2,1,0:T(8,128)(2,1)}, bf16[4,1,64,256]{3,2,1,0:T(8,128)(2,1)S(1)}, u32[]{:S(2)}) copy-start(bf16[4,1,64,256]{3,2,1,0:T(8,128)(2,1)S(1)} %collective-permute-done.4) | copy-start | bytes 393220
  57.7 19.5 %collective-permute-start.5 = (bf16[2,6,64,256]{3,2,1,0:T(8,128)(2,1)}, bf16[2,6,64,256]{3,2,1,0:T(8,128)(2,1)}, u32[]{:S(2)}, u32[]{:S(2)}) collective-permute-start(bf16[2,6,64,256]{3,2,1,0:T(8,128)(2,1)} %pad_maximum_fusion.7), channel_id=1, source_target_pairs={{0,8},{8,16},{16,24},{1,9},{9,17},{17,25},{2,10},{10,18},{18,26},{... | collective-permute-start | bytes 1179656 | tf_op jit(solution)/shard_map/ppermute | solution.py:28
  61.3 8.9 %collective-permute-start.10 = (bf16[4,1,64,256]{3,2,1,0:T(8,128)(2,1)}, bf16[4,1,64,256]{3,2,1,0:T(8,128)(2,1)S(1)}, u32[]{:S(2)}, u32[]{:S(2)}) collective-permute-start(bf16[4,1,64,256]{3,2,1,0:T(8,128)(2,1)} %get-tuple-element.8), channel_id=1, source_target_pairs={{1,0},{2,1},{3,2},{4,3},{5,4},{6,5},{7,6},{9,8},{10,9},{11,10},{12... | collective-permute-start | bytes 393224 | tf_op jit(solution)/shard_map/ppermute | solution.py:20
  62.6 11.5 %collective-permute-start.9 = (bf16[4,1,64,256]{3,2,1,0:T(8,128)(2,1)}, bf16[4,1,64,256]{3,2,1,0:T(8,128)(2,1)}, u32[]{:S(2)}, u32[]{:S(2)}) collective-permute-start(bf16[4,1,64,256]{3,2,1,0:T(8,128)(2,1)} %get-tuple-element.7), channel_id=1, source_target_pairs={{0,1},{1,2},{2,3},{3,4},{4,5},{5,6},{6,7},{8,9},{9,10},{10,11},{11... | collective-permute-start | bytes 393224 | tf_op jit(solution)/shard_map/ppermute | solution.py:17
  70.2 15.7 %copy-start.9 = (bf16[4,1,64,256]{3,2,1,0:T(8,128)(2,1)}, bf16[4,1,64,256]{3,2,1,0:T(8,128)(2,1)S(1)}, u32[]{:S(2)}) copy-start(bf16[4,1,64,256]{3,2,1,0:T(8,128)(2,1)S(1)} %collective-permute-done.10) | copy-start | bytes 393220
  75.7 42.2 %collective-permute-start.11 = (bf16[2,6,64,256]{3,2,1,0:T(8,128)(2,1)}, bf16[2,6,64,256]{3,2,1,0:T(8,128)(2,1)}, u32[]{:S(2)}, u32[]{:S(2)}) collective-permute-start(bf16[2,6,64,256]{3,2,1,0:T(8,128)(2,1)} %pad_maximum_fusion.5), channel_id=1, source_target_pairs={{8,0},{16,8},{24,16},{9,1},{17,9},{25,17},{10,2},{18,10},{26,18},{... | collective-permute-start | bytes 1179656 | tf_op jit(solution)/shard_map/ppermute | solution.py:28
  78.8 1.9 %copy-start.1 = (bf16[4,4,64,256]{3,2,1,0:T(8,128)(2,1)S(1)}, bf16[4,4,64,256]{3,2,1,0:T(8,128)(2,1)}, u32[]{:S(2)}) copy-start(bf16[4,4,64,256]{3,2,1,0:T(8,128)(2,1)} %param.9) | copy-start | bytes 1572868
  80.7 3.0 %copy-start = (bf16[6,4,576,256]{3,2,1,0:T(8,128)(2,1)}, bf16[6,4,576,256]{3,2,1,0:T(8,128)(2,1)S(1)}, u32[]{:S(2)}) copy-start(bf16[6,4,576,256]{3,2,1,0:T(8,128)(2,1)S(1)} %fusion.44) | copy-start | bytes 21233668
  119.2 2.2 %slice-start = ((s8[7077888]{0:T(1024)(128)(4,1)}), s8[4194304]{0:T(1024)(128)(4,1)S(1)}, s32[]{:S(2)}) async-start(s8[7077888]{0:T(1024)(128)(4,1)} %bitcast.195), calls=%async_computation | async-start | bytes 8388608
  119.5 1.9 %copy-start.5 = (bf16[64,3,3,64]{0,3,2,1:T(8,128)(2,1)S(1)}, bf16[64,3,3,64]{0,3,2,1:T(8,128)(2,1)}, u32[]{:S(2)}) copy-start(bf16[64,3,3,64]{0,3,2,1:T(8,128)(2,1)} %copy.30) | copy-start | bytes 221188
  120.3 2.3 %slice-start.1 = ((s8[7077888]{0:T(1024)(128)(4,1)}), s8[2883584]{0:T(1024)(128)(4,1)S(1)}, s32[]{:S(2)}) async-start(s8[7077888]{0:T(1024)(128)(4,1)} %bitcast.195), calls=%async_computation.1 | async-start | bytes 5767168
  120.4 3.3 %copy-start.8 = (bf16[1,3,3,64,64]{4,3,2,1,0:T(8,128)(2,1)S(1)}, bf16[1,3,3,64,64]{4,3,2,1,0:T(8,128)(2,1)}, u32[]{:S(2)}) copy-start(bf16[1,3,3,64,64]{4,3,2,1,0:T(8,128)(2,1)} %get-tuple-element.20) | copy-start | bytes 221188
  121.1 3.6 %copy-start.7 = (bf16[1,3,3,64,64]{4,3,2,1,0:T(8,128)(2,1)S(1)}, bf16[1,3,3,64,64]{4,3,2,1,0:T(8,128)(2,1)}, u32[]{:S(2)}) copy-start(bf16[1,3,3,64,64]{4,3,2,1,0:T(8,128)(2,1)} %get-tuple-element.19) | copy-start | bytes 221188
  123.6 2.2 %copy-start.6 = (bf16[1,3,3,64,64]{4,3,2,1,0:T(8,128)(2,1)S(1)}, bf16[1,3,3,64,64]{4,3,2,1,0:T(8,128)(2,1)}, u32[]{:S(2)}) copy-start(bf16[1,3,3,64,64]{4,3,2,1,0:T(8,128)(2,1)} %get-tuple-element.15) | copy-start | bytes 221188
  124.7 3.0 %copy-start.4 = (bf16[64,3,3,64]{0,3,2,1:T(8,128)(2,1)S(1)}, bf16[64,3,3,64]{0,3,2,1:T(8,128)(2,1)}, u32[]{:S(2)}) copy-start(bf16[64,3,3,64]{0,3,2,1:T(8,128)(2,1)} %copy.28) | copy-start | bytes 221188
  125.8 3.0 %copy-start.3 = (bf16[64,3,3,64]{0,3,2,1:T(8,128)(2,1)S(1)}, bf16[64,3,3,64]{0,3,2,1:T(8,128)(2,1)}, u32[]{:S(2)}) copy-start(bf16[64,3,3,64]{0,3,2,1:T(8,128)(2,1)} %copy.32) | copy-start | bytes 221188

commit v2 on v1

v2 whole, which is shorter than its diff:
```python
import functools
import math

import jax
import jax.numpy as jnp
from jax import lax
from jax.experimental import pallas as pl
from jax.experimental.pallas import tpu as pltpu
from jax.sharding import PartitionSpec as P

MESH = pl.DeviceIdType.MESH
LANES = 128


def remote(src, dst, send_sem, recv_sem, device):
    return pltpu.make_async_remote_copy(
        src_ref=src,
        dst_ref=dst,
        send_sem=send_sem,
        recv_sem=recv_sem,
        device_id=device,
        device_id_type=MESH,
    )


class Halo:
    def __init__(self, field, sems, later, sizes, place):
        self.field, self.later = field, later
        frames, rows = sizes
        f, r = place
        self.frame_count, self.row_count = field.shape[0] - 2, field.shape[1] - 2
        chan = self.chan = field.shape[2] // 3
        fc, rc = self.frame_count, self.row_count
        mid = pl.ds(chan, chan)
        self.first = 0 if later else 2
        local = pl.ds(self.first, fc)
        edge, rim = (pl.ds(0, 2), pl.ds(fc, 2)) if later else (pl.ds(fc, 2), pl.ds(0, 2))
        self.rim_first = fc if later else 0
        up, down = lax.rem(r + 1, rows), lax.rem(r + rows - 1, rows)
        side = lax.rem(f + (frames - 1 if later else 1), frames)
        to_up, to_down = r < rows - 1, r > 0
        to_side, from_side = (f > 0, f < frames - 1) if later else (f < frames - 1, f > 0)
        self.items = []
        plan = [
            (local, rc, local, 0, (f, up), to_up, to_down),
            (local, 1, local, rc + 1, (f, down), to_down, to_up),
            (edge, pl.ds(1, rc), rim, pl.ds(1, rc), (side, r), to_side, from_side),
            (edge, rc, rim, 0, (side, up), to_side & to_up, from_side & to_down),
            (edge, 1, rim, rc + 1, (side, down), to_side & to_down, from_side & to_up),
        ]
        for n, (se, sr, de, dr, device, sends, gets) in enumerate(plan):
            target = field.at[de, dr, mid]
            copy = remote(field.at[se, sr, mid], target, sems.at[0, n], sems.at[1, n], device)
            self.items.append((copy, target, sends, gets))

    def start(self):
        for copy, _, sends, _ in self.items:
            pl.when(sends)(copy.start)

    def shift(self, first, count, rows):
        field, chan = self.field, self.chan

        def body(e, carry):
            for row in rows:
                value = field[e, row, chan : 2 * chan].astype(jnp.float32)
                cols = value.shape[1]
                lane = lax.broadcasted_iota(jnp.int32, value.shape, 1)
                left = jnp.where(lane == 0, 0.0, pltpu.roll(value, 1, 1))
                right = jnp.where(lane == cols - 1, 0.0, pltpu.roll(value, cols - 1, 1))
                field[e, row, 0:chan] = left.astype(jnp.bfloat16)
                field[e, row, 2 * chan : 3 * chan] = right.astype(jnp.bfloat16)
            return carry

        lax.fori_loop(first, first + count, body, 0)

    def shift_local(self):
        self.shift(self.first, self.frame_count, range(1, self.row_count + 1))

    def finish(self):
        for copy, target, _, gets in self.items:
            pl.when(gets)(copy.wait_recv)

            def clear(target=target):
                target[...] = jnp.zeros(target.shape, jnp.bfloat16)

            pl.when(jnp.logical_not(gets))(clear)
        self.shift(self.first, self.frame_count, (0, self.row_count + 1))
        self.shift(self.rim_first, 2, range(self.row_count + 2))

    def drain(self):
        for copy, _, sends, _ in self.items:
            pl.when(sends)(copy.wait_send)


def offsets(e, frame_count):
    return max(0, e - frame_count + 1), min(2, e)


def convolve(field, weights, emit):
    frame_count, row_count = field.shape[0] - 2, field.shape[1] - 2
    chan, cols = field.shape[2] // 3, field.shape[3]

    def body(r, carry):
        sums = [None] * frame_count
        for e in range(frame_count + 2):
            low, high = offsets(e, frame_count)
            taps = field[e, pl.ds(r, 3)].reshape((9 * chan, cols))
            part = jnp.dot(
                weights[low * chan : (high + 1) * chan], taps, preferred_element_type=jnp.float32
            )
            for t in range(low, high + 1):
                term = part[(t - low) * chan : (t - low + 1) * chan]
                sums[e - t] = term if sums[e - t] is None else sums[e - t] + term
        for f in range(frame_count):
            emit(f, r, sums[f])
        return carry

    lax.fori_loop(0, row_count, body, 0)


def kernel_grad(upstream, field, total):
    frame_count, row_count = field.shape[0] - 2, field.shape[1] - 2
    chan, cols = field.shape[2] // 3, field.shape[3]
    total[...] = jnp.zeros(total.shape, jnp.float32)

    def body(r, carry):
        for e in range(frame_count + 2):
            low, high = offsets(e, frame_count)
            taps = field[e, pl.ds(r, 3)].reshape((9 * chan, cols))
            left = jnp.concatenate(
                [upstream[e - t, r + 1, chan : 2 * chan] for t in range(low, high + 1)], axis=0
            )
            part = lax.dot_general(
                left, taps, (((1,), (1,)), ((), ())), preferred_element_type=jnp.float32
            )
            total[low * chan : (high + 1) * chan, 0 : 9 * chan] += part
        return carry

    lax.fori_loop(0, row_count, body, 0)


def block_kernel(
    frames, rows, inv_scale,
    clip_ref, cot_ref, one_ref, two_ref, one_adj_ref, two_adj_ref, bias_ref,
    block_ref, input_ref, first_ref, second_ref, bias_out_ref,
    clip_f, cot_f, act_f, pre_f, slope, first_sum, second_sum, bias_sum,
    send, got_f, part, total, got_r, full,
    halo_sems, sems_f, sems_r, sems_gr, sems_gf,
):
    f, r = lax.axis_index("frames"), lax.axis_index("rows")
    frame_count, row_count, chan, cols = clip_ref.shape
    place, sizes = (f, r), (frames, rows)

    barrier = pltpu.get_barrier_semaphore()
    others = [(lax.rem(f + d, frames), r) for d in range(1, frames)]
    others += [(f, lax.rem(r + d, rows)) for d in range(1, rows)]
    for df in (1, frames - 1):
        for dr in (1, rows - 1):
            others.append((lax.rem(f + df, frames), lax.rem(r + dr, rows)))
    for device in others:
        pl.semaphore_signal(barrier, inc=1, device_id=device, device_id_type=MESH)
    mid = slice(chan, 2 * chan)
    clip_f[2 : frame_count + 2, 1 : row_count + 1, mid] = clip_ref[...]
    cot_f[0:frame_count, 1 : row_count + 1, mid] = cot_ref[...]
    pl.semaphore_wait(barrier, len(others))

    clip_h = Halo(clip_f, halo_sems.at[0], False, sizes, place)
    cot_h = Halo(cot_f, halo_sems.at[1], True, sizes, place)
    act_h = Halo(act_f, halo_sems.at[2], False, sizes, place)
    pre_h = Halo(pre_f, halo_sems.at[3], True, sizes, place)
    clip_h.start()
    cot_h.start()
    clip_h.shift_local()
    cot_h.shift_local()
    clip_h.finish()

    def emit_hidden(fr, rr, value):
        hidden = value + bias_ref[...]
        sig = 1.0 / (1.0 + jnp.exp(-hidden))
        act_f[fr + 2, rr + 1, mid] = (hidden * sig).astype(jnp.bfloat16)
        slope[fr, rr] = sig * (1.0 + hidden * (1.0 - sig))

    convolve(clip_f, one_ref, emit_hidden)
    act_h.start()
    act_h.shift_local()

    cot_h.finish()
    bias_sum[...] = jnp.zeros(bias_sum.shape, jnp.float32)

    def emit_pre(fr, rr, value):
        pre = (value * slope[fr, rr]).astype(jnp.bfloat16)
        pre_f[fr, rr + 1, mid] = pre
        bias_sum[...] += pre.astype(jnp.float32)

    convolve(cot_f, two_adj_ref, emit_pre)
    pre_h.start()
    pre_h.shift_local()

    act_h.finish()
    kernel_grad(cot_f, act_f, second_sum)
    kernel_grad(pre_f, clip_f, first_sum)

    wide = second_sum.shape[1] // LANES
    tall = second_sum.shape[0]
    half = wide * tall + chan
    for k, grad in enumerate((first_sum, second_sum)):
        for b in range(wide):
            send[pl.ds(k * half + b * tall, tall)] = grad[:, b * LANES : (b + 1) * LANES].astype(
                jnp.bfloat16
            )
    bias_term = jnp.sum(bias_sum[...], axis=1, keepdims=True)
    bias_rows = jnp.broadcast_to(bias_term, (chan, LANES)).astype(jnp.bfloat16)
    send[pl.ds(half - chan, chan)] = bias_rows
    send[pl.ds(2 * half - chan, chan)] = bias_rows
    count = send.shape[0]
    if count > 2 * half:
        send[pl.ds(2 * half, count - 2 * half)] = jnp.zeros((count - 2 * half, LANES), jnp.bfloat16)
    chunk_f = count // frames
    chunk_r = chunk_f // rows
    copies = []
    for d in range(1, frames):
        p = lax.rem(f + d, frames)
        at = pl.multiple_of(p * chunk_f, chunk_f)
        copies.append(
            remote(
                send.at[pl.ds(at, chunk_f)], got_f.at[d - 1],
                sems_f.at[0, d - 1], sems_f.at[1, d - 1], (p, r),
            )
        )
        copies[-1].start()

    def emit_block(fr, rr, value):
        block_ref[fr, rr] = (clip_ref[fr, rr].astype(jnp.float32) + value).astype(jnp.bfloat16)

    convolve(act_f, two_ref, emit_block)

    own_f = pl.multiple_of(f * chunk_f, chunk_f)
    total[...] = send[pl.ds(own_f, chunk_f)].astype(jnp.float32)
    for d in range(1, frames):
        copies[d - 1].wait_recv()
        total[...] += got_f[d - 1].astype(jnp.float32)
    part[...] = total[...].astype(jnp.bfloat16)
    for d in range(1, rows):
        q = lax.rem(r + d, rows)
        at = pl.multiple_of(q * chunk_r, chunk_r)
        copies.append(
            remote(
                part.at[pl.ds(at, chunk_r)], got_r.at[d - 1],
                sems_r.at[0, d - 1], sems_r.at[1, d - 1], (f, q),
            )
        )
        copies[-1].start()

    pre_h.finish()

    def emit_input(fr, rr, value):
        input_ref[fr, rr] = (cot_ref[fr, rr].astype(jnp.float32) + value).astype(jnp.bfloat16)

    convolve(pre_f, one_adj_ref, emit_input)

    mine = total[pl.ds(pl.multiple_of(r * chunk_r, chunk_r), chunk_r)]
    for d in range(1, rows):
        copies[frames - 2 + d].wait_recv()
        mine = mine + got_r[d - 1].astype(jnp.float32)
    here = pl.ds(pl.multiple_of(f * chunk_f + r * chunk_r, chunk_r), chunk_r)
    full[here] = mine.astype(jnp.bfloat16)
    gathers = []
    for d in range(1, rows):
        gathers.append(
            remote(
                full.at[here], full.at[here], sems_gr.at[0, d - 1], sems_gr.at[1, d - 1],
                (f, lax.rem(r + d, rows)),
            )
        )
        gathers[-1].start()
    for copy in gathers:
        copy.wait_recv()
    block = pl.ds(own_f, chunk_f)
    for d in range(1, frames):
        gathers.append(
            remote(
                full.at[block], full.at[block], sems_gf.at[0, d - 1], sems_gf.at[1, d - 1],
                (lax.rem(f + d, frames), r),
            )
        )
        gathers[-1].start()
    for copy in gathers[rows - 1 :]:
        copy.wait_recv()

    for k, out in enumerate((first_ref, second_ref)):
        for t in range(3):
            for tap in range(9):
                lane = tap * chan
                b, inner = lane // LANES, lane % LANES
                tile = full[pl.ds(k * half + b * tall + t * chan, chan)]
                out[t, tap // 3, tap % 3] = (
                    tile[:, inner : inner + chan].astype(jnp.float32) * inv_scale
                )
    bias_out_ref[...] = full[pl.ds(half - chan, chan)].astype(jnp.float32) * inv_scale
    for copy in copies + gathers:
        copy.wait_send()
    for halo in (clip_h, cot_h, act_h, pre_h):
        halo.drain()


def per_device(clip_in, kernel_one, bias_one, kernel_two, cotangent):
    frame_count, row_count, chan, cols = clip_in.shape
    frames, rows = lax.axis_size("frames"), lax.axis_size("rows")
    inv_scale = 1.0 / math.sqrt(frame_count * frames * row_count * rows * cols)

    def forward(kernel):
        return jnp.transpose(kernel, (0, 3, 1, 2, 4)).reshape((3 * chan, 9 * chan))

    def adjoint(kernel):
        flipped = jnp.flip(kernel, (0, 1, 2))
        return jnp.transpose(flipped, (0, 4, 1, 2, 3)).reshape((3 * chan, 9 * chan))

    wide = -(-9 * chan // LANES)
    tall = 3 * chan
    count = 2 * (wide * tall + chan)
    count += -count % (frames * rows * 16)
    chunk_f = count // frames
    chunk_r = chunk_f // rows
    dma = pltpu.SemaphoreType.DMA
    bf16, f32 = jnp.bfloat16, jnp.float32
    field = pltpu.VMEM((frame_count + 2, row_count + 2, 3 * chan, cols), bf16)
    vmem = pl.BlockSpec(memory_space=pltpu.VMEM)
    block, grad_input, first, second, bias = pl.pallas_call(
        functools.partial(block_kernel, frames, rows, inv_scale),
        out_shape=(
            jax.ShapeDtypeStruct(clip_in.shape, bf16),
            jax.ShapeDtypeStruct(clip_in.shape, bf16),
            jax.ShapeDtypeStruct(kernel_one.shape, f32),
            jax.ShapeDtypeStruct(kernel_two.shape, f32),
            jax.ShapeDtypeStruct((chan, LANES), f32),
        ),
        in_specs=[vmem] * 7,
        out_specs=(vmem,) * 5,
        scratch_shapes=[
            field, field, field, field,
            pltpu.VMEM(clip_in.shape, f32),
            pltpu.VMEM((tall, wide * LANES), f32),
            pltpu.VMEM((tall, wide * LANES), f32),
            pltpu.VMEM((chan, cols), f32),
            pltpu.VMEM((count, LANES), bf16),
            pltpu.VMEM((frames - 1, chunk_f, LANES), bf16),
            pltpu.VMEM((chunk_f, LANES), bf16),
            pltpu.VMEM((chunk_f, LANES), f32),
            pltpu.VMEM((rows - 1, chunk_r, LANES), bf16),
            pltpu.VMEM((count, LANES), bf16),
            dma((4, 2, 5)),
            dma((2, frames - 1)),
            dma((2, rows - 1)),
            dma((2, rows - 1)),
            dma((2, frames - 1)),
        ],
        compiler_params=pltpu.CompilerParams(
            collective_id=0, has_side_effects=True, vmem_limit_bytes=48 * 1024 * 1024
        ),
    )(
        clip_in, cotangent, forward(kernel_one), forward(kernel_two),
        adjoint(kernel_one), adjoint(kernel_two), bias_one.reshape((chan, 1)),
    )
    return block, grad_input, first, second, bias[:, 0]


def solution(mesh):
    in_specs = (P("frames", "rows", None, None), P(), P(), P(), P("frames", "rows", None, None))
    out_specs = (P("frames", "rows", None, None), P("frames", "rows", None, None), P(), P(), P())
    return jax.shard_map(
        per_device, mesh=mesh, in_specs=in_specs, out_specs=out_specs, check_vma=False
    )
```

time: 131 us -> 77.5 us (0.59)
  Pallas kernels: 27.7 us -> 63.8 us
  starting transfers between devices: 34.6 us -> 0 us
  matrix products: 23.6 us -> 0 us
  local copies, waits for them, and re-layouts: 26.1 us -> 11.9 us
  waiting for transfers between devices: 9.8 us -> 0 us
  other arithmetic: 7.42 us -> 0 us
    pallas_call x1, Pallas kernels: 27.7 us -> 63.8 us  [per_device(): pl.pallas_call(functools.partial(block_kernel, frames, rows, inv_scale),...]
    ppermute x12 -> x0, starting transfers between devices: 34.6 us -> none  [the longest x4 20.9 us: with_halo(): lax.ppermute(lax.slice_in_dim(block, block.shape[dim] - width, None, axis...]
    dot_general x18 -> x0, matrix products: 23.6 us -> none  [the longest x6 8.59 us: kernel_grad(): jnp.einsum('frow,frkw->ok', upstream, taps[t:t + frame_count], preferred_...]
    ppermute x12 -> x0, waiting for transfers between devices: 9.8 us -> none  [the longest x4 5.07 us: with_halo(): lax.ppermute(lax.slice_in_dim(block, 0, width, axis=dim), axis, backward)]
    slice x8 -> x1, local copies, waits for them, and re-layouts: 7.46 us -> 0.63 us  [per_device(): return (block, grad_input, first, second, bias[:, 0])]
    concatenate x6 -> x0, other arithmetic: 5.21 us -> none  [the longest x2 2.47 us: with_halo(): block = jnp.concatenate([low, block, high], axis=dim)]
    unnamed x62 -> x14, local copies, waits for them, and re-layouts: 10 us -> 5.95 us
    mul x2 -> x0, local copies, waits for them, and re-layouts: 2.24 us -> none  [the longest x1 1.12 us: per_device(): total_first * inv_scale]
  transfers between devices with their start and end apart: 12 -> 0, of which waited for: 3 -> 0; matrix products, arithmetic and copies ran while one was open for 25% -> 0% of each run, Pallas kernels for 21% -> 0%
where the time goes in v2:
time: 77.5 us; the launch traced here: 76.5 us
  Pallas kernels  63.8 us (82%)
  local copies, waits for them, and re-layouts  11.9 us (15%)
    pallas_call x1, Pallas kernels, per_device(): pl.pallas_call(functools.partial(block_kernel, frames, rows, inv_scale),...  63.8 us
    unnamed x14, local copies, waits for them, and re-layouts  5.95 us
    transpose x4, local copies, waits for them, and re-layouts, adjoint(): return jnp.transpose(flipped, (0, 4, 1, 2, 3)).reshape((3 * chan, 9 * chan))  2.94 us

profile of v2, /device:TPU:0, one launch (start us, length us, event | category | flops | bytes accessed | tf_op | source)
XLA Modules:
  0.0 76.5 jit_solution(8237645403338565872)
XLA Ops:
  0.6 0.0 copy-start.4
  0.6 0.6 copy-done.4
  1.3 0.1 copy.19.bias_ref
  1.4 1.0 %reverse_bitcast_fusion.1 = bf16[3,64,3,3,64]{1,4,3,2,0:T(8,128)(2,1)S(1)} fusion(bf16[3,3,3,64,64]{4,3,2,1,0:T(8,128)(2,1)} %param.6), kind=kLoop, calls=%fused_computation.1 | loop fusion | bytes 442368 | tf_op jit(solution)/shard_map/transpose | solution.py:316
  2.4 0.9 %copy.17 = bf16[3,64,3,3,64]{4,3,2,1,0:T(4,128)(2,1)S(1)} copy(bf16[3,64,3,3,64]{1,4,3,2,0:T(8,128)(2,1)S(1)} %reverse_bitcast_fusion.1) | data formatting | bytes 442368 | tf_op jit(solution)/shard_map/transpose | solution.py:316
  3.4 0.0 copy-start.2
  3.4 0.4 reshape.27.one_adj_ref
  3.8 0.6 copy-done.2
  4.4 0.9 %copy.18 = bf16[3,64,3,3,64]{4,3,2,1,0:T(4,128)(2,1)S(1)} copy(bf16[3,64,3,3,64]{1,4,3,2,0:T(8,128)(2,1)S(1)} %reverse_bitcast_fusion) | data formatting | bytes 442368 | tf_op jit(solution)/shard_map/transpose | solution.py:316
  5.4 0.4 reshape.28.two_adj_ref
  5.8 0.4 copy.16
  6.2 0.0 copy-start.3
  6.2 0.4 reshape.26.two_ref
  6.6 0.6 copy-done.3
  7.2 0.0 copy-start.1
  7.2 0.4 copy.15
  7.6 0.0 copy-start
  7.6 0.4 reshape.25.one_ref
  8.0 0.2 copy-done.1
  8.2 0.4 copy-done
  8.6 63.8 %shard_map.92 = (bf16[4,4,64,256]{3,2,1,0:T(8,128)(2,1)S(1)}, bf16[4,4,64,256]{3,2,1,0:T(8,128)(2,1)S(1)}, f32[3,3,3,64,64]{4,3,2,1,0:T(8,128)S(1)}, f32[3,3,3,64,64]{4,3,2,1,0:T(8,128)S(1)}, f32[64,128]{1,0:T(8,128)S(1)}) custom-call(bf16[4,4,64,256]{3,2,1,0:T(8,128)(2,1)S(1)} %copy-done, bf16[4,4,64,256]{3,2,1,0:T(8,128)(2,1)S(1)} %copy-done.1, ...), custom_call_target="tpu_custom_call" | custom-call | tf_op jit(solution)/shard_map/pallas_call | solution.py:328
  72.4 0.6 slice_reduce_fusion
  73.1 0.8 %copy.24 = bf16[4,4,64,256]{3,2,1,0:T(8,128)(2,1)} copy(bf16[4,4,64,256]{3,2,1,0:T(8,128)(2,1)S(1)} %get-tuple-element.20) | data formatting | bytes 1048576
  73.9 0.8 %copy.25 = bf16[4,4,64,256]{3,2,1,0:T(8,128)(2,1)} copy(bf16[4,4,64,256]{3,2,1,0:T(8,128)(2,1)S(1)} %get-tuple-element.21) | data formatting | bytes 1048576
  74.7 0.9 %copy.26 = f32[3,3,3,64,64]{4,3,2,1,0:T(8,128)} copy(f32[3,3,3,64,64]{4,3,2,1,0:T(8,128)S(1)} %get-tuple-element.22) | data formatting | bytes 884736
  75.6 0.9 %copy.27 = f32[3,3,3,64,64]{4,3,2,1,0:T(8,128)} copy(f32[3,3,3,64,64]{4,3,2,1,0:T(8,128)S(1)} %get-tuple-element.23) | data formatting | bytes 884736
  (1 shorter events, 0.0 us)
Async XLA Ops:
  0.6 0.7 copy-start.4
  3.4 1.0 %copy-start.2 = (bf16[3,3,3,64,64]{4,3,2,1,0:T(8,128)(2,1)S(1)}, bf16[3,3,3,64,64]{4,3,2,1,0:T(8,128)(2,1)}, u32[]{:S(2)}) copy-start(bf16[3,3,3,64,64]{4,3,2,1,0:T(8,128)(2,1)} %param.8) | copy-start | bytes 663556
  6.2 1.0 %copy-start.3 = (bf16[3,3,3,64,64]{4,3,2,1,0:T(8,128)(2,1)S(1)}, bf16[3,3,3,64,64]{4,3,2,1,0:T(8,128)(2,1)}, u32[]{:S(2)}) copy-start(bf16[3,3,3,64,64]{4,3,2,1,0:T(8,128)(2,1)} %param.6) | copy-start | bytes 663556
  7.2 1.0 %copy-start.1 = (bf16[4,4,64,256]{3,2,1,0:T(8,128)(2,1)S(1)}, bf16[4,4,64,256]{3,2,1,0:T(8,128)(2,1)}, u32[]{:S(2)}) copy-start(bf16[4,4,64,256]{3,2,1,0:T(8,128)(2,1)} %cot_ref.1) | copy-start | bytes 1572868
  7.6 1.1 %copy-start = (bf16[4,4,64,256]{3,2,1,0:T(8,128)(2,1)S(1)}, bf16[4,4,64,256]{3,2,1,0:T(8,128)(2,1)}, u32[]{:S(2)}) copy-start(bf16[4,4,64,256]{3,2,1,0:T(8,128)(2,1)} %clip_ref.1) | copy-start | bytes 1572868

commit v3 on v2

v3 whole, which is shorter than its diff:
```python
import functools
import math

import jax
import jax.numpy as jnp
from jax import lax
from jax.experimental import pallas as pl
from jax.experimental.pallas import tpu as pltpu
from jax.sharding import PartitionSpec as P

MESH = pl.DeviceIdType.MESH
LANES = 128


def remote(src, dst, send_sem, recv_sem, device):
    return pltpu.make_async_remote_copy(
        src_ref=src,
        dst_ref=dst,
        send_sem=send_sem,
        recv_sem=recv_sem,
        device_id=device,
        device_id_type=MESH,
    )


class Halo:
    def __init__(self, field, sems, later, sizes, place):
        self.field, self.later = field, later
        frames, rows = sizes
        f, r = place
        self.frame_count, self.row_count = field.shape[0] - 2, field.shape[1] - 2
        chan = self.chan = field.shape[2] // 3
        fc, rc = self.frame_count, self.row_count
        mid = pl.ds(chan, chan)
        self.first = 0 if later else 2
        local = pl.ds(self.first, fc)
        edge, rim = (pl.ds(0, 2), pl.ds(fc, 2)) if later else (pl.ds(fc, 2), pl.ds(0, 2))
        self.rim_first = fc if later else 0
        up, down = lax.rem(r + 1, rows), lax.rem(r + rows - 1, rows)
        side = lax.rem(f + (frames - 1 if later else 1), frames)
        to_up, to_down = r < rows - 1, r > 0
        to_side, from_side = (f > 0, f < frames - 1) if later else (f < frames - 1, f > 0)
        self.items = []
        plan = [
            (local, rc, local, 0, (f, up), to_up, to_down),
            (local, 1, local, rc + 1, (f, down), to_down, to_up),
            (edge, pl.ds(1, rc), rim, pl.ds(1, rc), (side, r), to_side, from_side),
            (edge, rc, rim, 0, (side, up), to_side & to_up, from_side & to_down),
            (edge, 1, rim, rc + 1, (side, down), to_side & to_down, from_side & to_up),
        ]
        for n, (se, sr, de, dr, device, sends, gets) in enumerate(plan):
            target = field.at[de, dr, mid]
            copy = remote(field.at[se, sr, mid], target, sems.at[0, n], sems.at[1, n], device)
            self.items.append((copy, target, sends, gets))

    def start(self):
        for copy, _, sends, _ in self.items:
            pl.when(sends)(copy.start)

    def shift(self, first, count, rows):
        field, chan = self.field, self.chan

        def body(e, carry):
            for row in rows:
                value = field[e, row, chan : 2 * chan].astype(jnp.float32)
                cols = value.shape[1]
                lane = lax.broadcasted_iota(jnp.int32, value.shape, 1)
                left = jnp.where(lane == 0, 0.0, pltpu.roll(value, 1, 1))
                right = jnp.where(lane == cols - 1, 0.0, pltpu.roll(value, cols - 1, 1))
                field[e, row, 0:chan] = left.astype(jnp.bfloat16)
                field[e, row, 2 * chan : 3 * chan] = right.astype(jnp.bfloat16)
            return carry

        lax.fori_loop(first, first + count, body, 0)

    def shift_local(self):
        self.shift(self.first, self.frame_count, range(1, self.row_count + 1))

    def receive(self):
        for copy, target, _, gets in self.items:
            pl.when(gets)(copy.wait_recv)

            def clear(target=target):
                target[...] = jnp.zeros(target.shape, jnp.bfloat16)

            pl.when(jnp.logical_not(gets))(clear)

    def shift_rim(self):
        self.shift(self.first, self.frame_count, (0, self.row_count + 1))
        self.shift(self.rim_first, 2, range(self.row_count + 2))

    def drain(self):
        for copy, _, sends, _ in self.items:
            pl.when(sends)(copy.wait_send)


def offsets(e, frame_count):
    return max(0, e - frame_count + 1), min(2, e)


def convolve(field, weights, emit, start=0, stop=None):
    frame_count, row_count = field.shape[0] - 2, field.shape[1] - 2
    chan, cols = field.shape[2] // 3, field.shape[3]

    def body(r, carry):
        sums = [None] * frame_count
        for e in range(frame_count + 2):
            low, high = offsets(e, frame_count)
            taps = field[e, pl.ds(r, 3)].reshape((9 * chan, cols))
            part = jnp.dot(
                weights[low * chan : (high + 1) * chan, 0 : 9 * chan],
                taps,
                preferred_element_type=jnp.float32,
            )
            for t in range(low, high + 1):
                term = part[(t - low) * chan : (t - low + 1) * chan]
                sums[e - t] = term if sums[e - t] is None else sums[e - t] + term
        for f in range(frame_count):
            emit(f, r, sums[f])
        return carry

    lax.fori_loop(start, row_count if stop is None else stop, body, 0)


def kernel_grad(upstream, field, total):
    frame_count, row_count = field.shape[0] - 2, field.shape[1] - 2
    chan, cols = field.shape[2] // 3, field.shape[3]
    total[...] = jnp.zeros(total.shape, jnp.float32)
    blank = jnp.zeros((chan, row_count * cols), jnp.bfloat16)
    for e in range(frame_count + 2):
        low, high = offsets(e, frame_count)
        taps = jnp.concatenate(
            [field[e, r : r + 3].reshape((9 * chan, cols)) for r in range(row_count)], axis=1
        )
        right = []
        for t in range(3):
            if low <= t <= high:
                lines = [upstream[e - t, r + 1, chan : 2 * chan] for r in range(row_count)]
                right.append(jnp.concatenate(lines, axis=1))
            else:
                right.append(blank)
        total[0 : 9 * chan, 0 : 3 * chan] += lax.dot_general(
            taps,
            jnp.concatenate(right, axis=0),
            (((1,), (1,)), ((), ())),
            preferred_element_type=jnp.float32,
        )


def lay_forward(kernel, weights):
    chan = kernel.shape[3]
    for t in range(3):
        for tap in range(9):
            weights[t * chan : (t + 1) * chan, tap * chan : (tap + 1) * chan] = kernel[
                t, tap // 3, tap % 3
            ]


def lay_adjoint(kernel, weights):
    chan = kernel.shape[3]
    for t in range(3):
        for tap in range(9):
            piece = kernel[2 - t, 2 - tap // 3, 2 - tap % 3].astype(jnp.float32)
            weights[t * chan : (t + 1) * chan, tap * chan : (tap + 1) * chan] = jnp.transpose(
                piece
            ).astype(jnp.bfloat16)


class Reduction:
    def __init__(self, bufs, sems, sizes, place):
        self.send, self.got_f, self.part, self.total, self.got_r, self.full = bufs
        self.sems = sems
        self.sizes, self.place = sizes, place
        frames, rows = sizes
        f, r = place
        self.chunk_f = self.send.shape[0] // frames
        self.chunk_r = self.chunk_f // rows
        self.own_f = pl.multiple_of(f * self.chunk_f, self.chunk_f)
        self.frame_peers = [lax.rem(f + d, frames) for d in range(1, frames)]
        self.row_peers = [lax.rem(r + d, rows) for d in range(1, rows)]

    def copy(self, src, dst, kind, n, device):
        return remote(src, dst, self.sems.at[kind, 0, n], self.sems.at[kind, 1, n], device)

    def scatter_frames(self):
        _, r = self.place
        self.first = []
        for n, p in enumerate(self.frame_peers):
            at = pl.ds(pl.multiple_of(p * self.chunk_f, self.chunk_f), self.chunk_f)
            self.first.append(self.copy(self.send.at[at], self.got_f.at[n], 0, n, (p, r)))
            self.first[-1].start()

    def scatter_rows(self):
        f, _ = self.place
        value = self.send[pl.ds(self.own_f, self.chunk_f)].astype(jnp.float32)
        for n, copy in enumerate(self.first):
            copy.wait_recv()
            value = value + self.got_f[n].astype(jnp.float32)
        self.total[...] = value
        self.part[...] = value.astype(jnp.bfloat16)
        self.second = []
        for n, q in enumerate(self.row_peers):
            at = pl.ds(pl.multiple_of(q * self.chunk_r, self.chunk_r), self.chunk_r)
            self.second.append(self.copy(self.part.at[at], self.got_r.at[n], 1, n, (f, q)))
            self.second[-1].start()

    def gather_rows(self):
        f, r = self.place
        own = pl.multiple_of(r * self.chunk_r, self.chunk_r)
        value = self.total[pl.ds(own, self.chunk_r)]
        for n, copy in enumerate(self.second):
            copy.wait_recv()
            value = value + self.got_r[n].astype(jnp.float32)
        at = pl.multiple_of(f * self.chunk_f + r * self.chunk_r, self.chunk_r)
        here = self.full.at[pl.ds(at, self.chunk_r)]
        here[...] = value.astype(jnp.bfloat16)
        self.third = []
        for n, q in enumerate(self.row_peers):
            self.third.append(self.copy(here, here, 2, n, (f, q)))
            self.third[-1].start()

    def gather_frames(self):
        _, r = self.place
        for copy in self.third:
            copy.wait_recv()
        block = self.full.at[pl.ds(self.own_f, self.chunk_f)]
        self.fourth = []
        for n, p in enumerate(self.frame_peers):
            self.fourth.append(self.copy(block, block, 3, n, (p, r)))
            self.fourth[-1].start()

    def finish(self):
        for copy in self.fourth:
            copy.wait_recv()

    def drain(self):
        for copy in self.first + self.second + self.third + self.fourth:
            copy.wait_send()


def block_kernel(
    frames, rows, inv_scale,
    clip_ref, cot_ref, one_ref, two_ref, bias_ref,
    block_ref, input_ref, first_ref, second_ref, bias_out_ref,
    clip_f, cot_f, act_f, pre_f, slope, one_w, two_w, one_adj, two_adj, grad_sum, bias_sum,
    send, got_f, part, total, got_r, full,
    halo_sems, reduce_sems,
):
    f, r = lax.axis_index("frames"), lax.axis_index("rows")
    frame_count, row_count, chan, cols = clip_ref.shape
    place, sizes = (f, r), (frames, rows)

    barrier = pltpu.get_barrier_semaphore()
    others = [(lax.rem(f + d, frames), r) for d in range(1, frames)]
    others += [(f, lax.rem(r + d, rows)) for d in range(1, rows)]
    for df in (1, frames - 1):
        for dr in (1, rows - 1):
            others.append((lax.rem(f + df, frames), lax.rem(r + dr, rows)))
    for device in others:
        pl.semaphore_signal(barrier, inc=1, device_id=device, device_id_type=MESH)
    mid = slice(chan, 2 * chan)
    clip_f[2 : frame_count + 2, 1 : row_count + 1, mid] = clip_ref[...]
    cot_f[0:frame_count, 1 : row_count + 1, mid] = cot_ref[...]
    pl.semaphore_wait(barrier, len(others))

    clip_h = Halo(clip_f, halo_sems.at[0], False, sizes, place)
    cot_h = Halo(cot_f, halo_sems.at[1], True, sizes, place)
    act_h = Halo(act_f, halo_sems.at[2], False, sizes, place)
    pre_h = Halo(pre_f, halo_sems.at[3], True, sizes, place)
    clip_h.start()
    lay_forward(one_ref, one_w)
    clip_h.shift_local()
    lay_adjoint(two_ref, two_adj)
    clip_h.receive()
    cot_h.start()
    clip_h.shift_rim()

    def emit_hidden(fr, rr, value):
        hidden = value + bias_ref[...]
        sig = 1.0 / (1.0 + jnp.exp(-hidden))
        act_f[fr + 2, rr + 1, mid] = (hidden * sig).astype(jnp.bfloat16)
        slope[fr, rr] = sig * (1.0 + hidden * (1.0 - sig))

    convolve(clip_f, one_w, emit_hidden)
    act_h.start()
    cot_h.shift_local()
    act_h.shift_local()

    cot_h.receive()
    cot_h.shift_rim()
    bias_sum[...] = jnp.zeros(bias_sum.shape, jnp.float32)

    def emit_pre(fr, rr, value):
        pre = (value * slope[fr, rr]).astype(jnp.bfloat16)
        pre_f[fr, rr + 1, mid] = pre
        bias_sum[...] += pre.astype(jnp.float32)

    convolve(cot_f, two_adj, emit_pre)
    pre_h.start()

    wide = one_w.shape[1] // LANES
    tall = one_w.shape[0]
    used = wide * tall + chan
    reductions = [
        Reduction(
            [buf.at[k] for buf in (send, got_f, part, total, got_r, full)],
            reduce_sems.at[k], sizes, place,
        )
        for k in range(2)
    ]
    bias_term = jnp.sum(bias_sum[...], axis=1, keepdims=True)
    bias_rows = jnp.broadcast_to(bias_term, (chan, LANES)).astype(jnp.bfloat16)
    rest = send.shape[1] - used

    def reduce_grad(k):
        flipped = jnp.transpose(grad_sum[...])
        for b in range(wide):
            send[k, pl.ds(b * tall, tall)] = flipped[:tall, b * LANES : (b + 1) * LANES].astype(
                jnp.bfloat16
            )
        send[k, pl.ds(used - chan, chan)] = bias_rows
        if rest:
            send[k, pl.ds(used, rest)] = jnp.zeros((rest, LANES), jnp.bfloat16)
        reductions[k].scatter_frames()

    kernel_grad(pre_f, clip_f, grad_sum)
    reduce_grad(0)
    act_h.receive()
    act_h.shift_rim()
    kernel_grad(cot_f, act_f, grad_sum)
    reduce_grad(1)
    lay_forward(two_ref, two_w)
    lay_adjoint(one_ref, one_adj)
    pre_h.shift_local()

    def emit_block(fr, rr, value):
        block_ref[fr, rr] = (clip_ref[fr, rr].astype(jnp.float32) + value).astype(jnp.bfloat16)

    half_way = row_count // 2
    convolve(act_f, two_w, emit_block, 0, half_way)
    reductions[0].scatter_rows()
    convolve(act_f, two_w, emit_block, half_way, row_count)
    reductions[1].scatter_rows()

    pre_h.receive()
    pre_h.shift_rim()

    def emit_input(fr, rr, value):
        input_ref[fr, rr] = (cot_ref[fr, rr].astype(jnp.float32) + value).astype(jnp.bfloat16)

    convolve(pre_f, one_adj, emit_input, 0, 1)
    reductions[0].gather_rows()
    reductions[1].gather_rows()
    convolve(pre_f, one_adj, emit_input, 1, half_way)
    reductions[0].gather_frames()
    reductions[1].gather_frames()
    convolve(pre_f, one_adj, emit_input, half_way, row_count)

    for k, out in enumerate((first_ref, second_ref)):
        reductions[k].finish()
        for t in range(3):
            for tap in range(9):
                lane = tap * chan
                b, inner = lane // LANES, lane % LANES
                tile = full[k, pl.ds(b * tall + t * chan, chan)]
                out[t, tap // 3, tap % 3] = (
                    tile[:, inner : inner + chan].astype(jnp.float32) * inv_scale
                )
    bias_out_ref[...] = full[0, pl.ds(used - chan, chan)].astype(jnp.float32) * inv_scale
    for reduction in reductions:
        reduction.drain()
    for halo in (clip_h, cot_h, act_h, pre_h):
        halo.drain()


def per_device(clip_in, kernel_one, bias_one, kernel_two, cotangent):
    frame_count, row_count, chan, cols = clip_in.shape
    frames, rows = lax.axis_size("frames"), lax.axis_size("rows")
    inv_scale = 1.0 / math.sqrt(frame_count * frames * row_count * rows * cols)

    wide = -(-9 * chan // LANES)
    tall = 3 * chan
    count = wide * tall + chan
    count += -count % (frames * rows * 16)
    chunk_f = count // frames
    chunk_r = chunk_f // rows
    dma = pltpu.SemaphoreType.DMA
    bf16, f32 = jnp.bfloat16, jnp.float32
    field = pltpu.VMEM((frame_count + 2, row_count + 2, 3 * chan, cols), bf16)
    weights = pltpu.VMEM((tall, wide * LANES), bf16)
    vmem = pl.BlockSpec(memory_space=pltpu.VMEM)
    block, grad_input, first, second, bias = pl.pallas_call(
        functools.partial(block_kernel, frames, rows, inv_scale),
        out_shape=(
            jax.ShapeDtypeStruct(clip_in.shape, bf16),
            jax.ShapeDtypeStruct(clip_in.shape, bf16),
            jax.ShapeDtypeStruct(kernel_one.shape, f32),
            jax.ShapeDtypeStruct(kernel_two.shape, f32),
            jax.ShapeDtypeStruct((chan, LANES), f32),
        ),
        in_specs=[vmem] * 5,
        out_specs=(vmem,) * 5,
        scratch_shapes=[
            field, field, field, field,
            pltpu.VMEM(clip_in.shape, f32),
            weights, weights, weights, weights,
            pltpu.VMEM((wide * LANES, -(-tall // LANES) * LANES), f32),
            pltpu.VMEM((chan, cols), f32),
            pltpu.VMEM((2, count, LANES), bf16),
            pltpu.VMEM((2, frames - 1, chunk_f, LANES), bf16),
            pltpu.VMEM((2, chunk_f, LANES), bf16),
            pltpu.VMEM((2, chunk_f, LANES), f32),
            pltpu.VMEM((2, rows - 1, chunk_r, LANES), bf16),
            pltpu.VMEM((2, count, LANES), bf16),
            dma((4, 2, 5)),
            dma((2, 4, 2, max(frames, rows) - 1)),
        ],
        compiler_params=pltpu.CompilerParams(
            collective_id=0, has_side_effects=True, vmem_limit_bytes=48 * 1024 * 1024
        ),
    )(
        clip_in, cotangent, kernel_one, kernel_two, bias_one.reshape((chan, 1)),
    )
    return block, grad_input, first, second, bias[:, 0]


def solution(mesh):
    in_specs = (P("frames", "rows", None, None), P(), P(), P(), P("frames", "rows", None, None))
    out_specs = (P("frames", "rows", None, None), P("frames", "rows", None, None), P(), P(), P())
    return jax.shard_map(
        per_device, mesh=mesh, in_specs=in_specs, out_specs=out_specs, check_vma=False
    )
```

time: 77.5 us -> 69.3 us (0.89)
  Pallas kernels: 63.8 us -> 59.5 us
  local copies, waits for them, and re-layouts: 11.9 us -> 8.88 us
    pallas_call x1, Pallas kernels: 63.8 us -> 59.5 us  [per_device(): pl.pallas_call(functools.partial(block_kernel, frames, rows, inv_scale),...]
    transpose x6 -> x0, local copies, waits for them, and re-layouts: 3.7 us -> none  [the longest x4 2.94 us: adjoint(): return jnp.transpose(flipped, (0, 4, 1, 2, 3)).reshape((3 * chan, 9 * chan))]
    unnamed x14, local copies, waits for them, and re-layouts: 5.95 us -> 8.16 us
    reshape x4 -> x0, local copies, waits for them, and re-layouts: 1.57 us -> none  [the longest x2 0.78 us: forward(): return jnp.transpose(kernel, (0, 3, 1, 2, 4)).reshape((3 * chan, 9 * chan))]
where the time goes in v3:
time: 69.3 us; the launch traced here: 69 us
  Pallas kernels  59.5 us (86%)
  local copies, waits for them, and re-layouts  8.88 us (13%)
    pallas_call x1, Pallas kernels, per_device(): pl.pallas_call(functools.partial(block_kernel, frames, rows, inv_scale),...  59.5 us
    unnamed x14, local copies, waits for them, and re-layouts  8.16 us

profile of v3, /device:TPU:0, one launch (start us, length us, event | category | flops | bytes accessed | tf_op | source)
XLA Modules:
  0.0 69.0 jit_solution(4930939843552081890)
XLA Ops:
  0.6 0.0 copy-start.4
  0.6 0.6 copy-done.4
  1.3 0.1 copy.11.bias_ref
  1.4 0.0 copy-start
  1.4 1.0 %copy-done = bf16[4,4,64,256]{3,2,1,0:T(8,128)(2,1)S(1)} copy-done((bf16[4,4,64,256]{3,2,1,0:T(8,128)(2,1)S(1)}, bf16[4,4,64,256]{3,2,1,0:T(8,128)(2,1)}, u32[]{:S(2)}) %copy-start) | copy-done | bytes 524312
  2.4 0.0 copy-start.1
  2.4 1.0 %copy-done.1 = bf16[4,4,64,256]{3,2,1,0:T(8,128)(2,1)S(1)} copy-done((bf16[4,4,64,256]{3,2,1,0:T(8,128)(2,1)S(1)}, bf16[4,4,64,256]{3,2,1,0:T(8,128)(2,1)}, u32[]{:S(2)}) %copy-start.1) | copy-done | bytes 524312
  3.5 0.0 copy-start.2
  3.5 1.0 %copy-done.2 = bf16[3,3,3,64,64]{4,3,2,1,0:T(8,128)(2,1)S(1)} copy-done((bf16[3,3,3,64,64]{4,3,2,1,0:T(8,128)(2,1)S(1)}, bf16[3,3,3,64,64]{4,3,2,1,0:T(8,128)(2,1)}, u32[]{:S(2)}) %copy-start.2) | copy-done | bytes 221208
  4.5 0.0 copy-start.3
  4.5 1.0 %copy-done.3 = bf16[3,3,3,64,64]{4,3,2,1,0:T(8,128)(2,1)S(1)} copy-done((bf16[3,3,3,64,64]{4,3,2,1,0:T(8,128)(2,1)S(1)}, bf16[3,3,3,64,64]{4,3,2,1,0:T(8,128)(2,1)}, u32[]{:S(2)}) %copy-start.3) | copy-done | bytes 221208
  5.5 59.5 %shard_map.92 = (bf16[4,4,64,256]{3,2,1,0:T(8,128)(2,1)S(1)}, bf16[4,4,64,256]{3,2,1,0:T(8,128)(2,1)S(1)}, f32[3,3,3,64,64]{4,3,2,1,0:T(8,128)S(1)}, f32[3,3,3,64,64]{4,3,2,1,0:T(8,128)S(1)}, f32[64,128]{1,0:T(8,128)S(1)}) custom-call(bf16[4,4,64,256]{3,2,1,0:T(8,128)(2,1)S(1)} %copy-done, bf16[4,4,64,256]{3,2,1,0:T(8,128)(2,1)S(1)} %copy-done.1, ...), custom_call_target="tpu_custom_call" | custom-call | tf_op jit(solution)/shard_map/pallas_call | solution.py:392
  65.0 0.6 slice_reduce_fusion
  65.6 0.8 %copy.16 = bf16[4,4,64,256]{3,2,1,0:T(8,128)(2,1)} copy(bf16[4,4,64,256]{3,2,1,0:T(8,128)(2,1)S(1)} %get-tuple-element.20) | data formatting | bytes 1048576
  66.4 0.8 %copy.17 = bf16[4,4,64,256]{3,2,1,0:T(8,128)(2,1)} copy(bf16[4,4,64,256]{3,2,1,0:T(8,128)(2,1)S(1)} %get-tuple-element.21) | data formatting | bytes 1048576
  67.2 0.9 %copy.18 = f32[3,3,3,64,64]{4,3,2,1,0:T(8,128)} copy(f32[3,3,3,64,64]{4,3,2,1,0:T(8,128)S(1)} %get-tuple-element.22) | data formatting | bytes 884736
  68.1 0.9 %copy.19 = f32[3,3,3,64,64]{4,3,2,1,0:T(8,128)} copy(f32[3,3,3,64,64]{4,3,2,1,0:T(8,128)S(1)} %get-tuple-element.23) | data formatting | bytes 884736
Async XLA Ops:
  0.6 0.7 copy-start.4
  1.4 1.0 %copy-start = (bf16[4,4,64,256]{3,2,1,0:T(8,128)(2,1)S(1)}, bf16[4,4,64,256]{3,2,1,0:T(8,128)(2,1)}, u32[]{:S(2)}) copy-start(bf16[4,4,64,256]{3,2,1,0:T(8,128)(2,1)} %clip_ref.1) | copy-start | bytes 1572868
  2.4 1.0 %copy-start.1 = (bf16[4,4,64,256]{3,2,1,0:T(8,128)(2,1)S(1)}, bf16[4,4,64,256]{3,2,1,0:T(8,128)(2,1)}, u32[]{:S(2)}) copy-start(bf16[4,4,64,256]{3,2,1,0:T(8,128)(2,1)} %cot_ref.1) | copy-start | bytes 1572868
  3.5 1.0 %copy-start.2 = (bf16[3,3,3,64,64]{4,3,2,1,0:T(8,128)(2,1)S(1)}, bf16[3,3,3,64,64]{4,3,2,1,0:T(8,128)(2,1)}, u32[]{:S(2)}) copy-start(bf16[3,3,3,64,64]{4,3,2,1,0:T(8,128)(2,1)} %one_ref.1) | copy-start | bytes 663556
  4.5 1.0 %copy-start.3 = (bf16[3,3,3,64,64]{4,3,2,1,0:T(8,128)(2,1)S(1)}, bf16[3,3,3,64,64]{4,3,2,1,0:T(8,128)(2,1)}, u32[]{:S(2)}) copy-start(bf16[3,3,3,64,64]{4,3,2,1,0:T(8,128)(2,1)} %two_ref.1) | copy-start | bytes 663556

commit v4 on v3

--- a/solution.py
+++ b/solution.py
@@ -98,13 +98,15 @@
     return max(0, e - frame_count + 1), min(2, e)
 
 
-def convolve(field, weights, emit, start=0, stop=None):
-    frame_count, row_count = field.shape[0] - 2, field.shape[1] - 2
+def convolve(field, weights, emit, rows, frames=None, base=None):
+    frame_count = field.shape[0] - 2
     chan, cols = field.shape[2] // 3, field.shape[3]
-
-    def body(r, carry):
-        sums = [None] * frame_count
-        for e in range(frame_count + 2):
+    start, count, step = rows
+
+    def body(k, carry):
+        r = start + k * step
+        sums = [None if base is None else base[f, r] for f in range(frame_count)]
+        for e in range(frame_count + 2) if frames is None else frames:
             low, high = offsets(e, frame_count)
             taps = field[e, pl.ds(r, 3)].reshape((9 * chan, cols))
             part = jnp.dot(
@@ -119,7 +121,25 @@
             emit(f, r, sums[f])
         return carry
 
-    lax.fori_loop(start, row_count if stop is None else stop, body, 0)
+    lax.fori_loop(0, count, body, 0)
+
+
+def convolve_local(field, weights, first, partial):
+    frame_count, row_count = field.shape[0] - 2, field.shape[1] - 2
+
+    def keep(f, r, value):
+        partial[f, r] = value
+
+    convolve(
+        field, weights, keep, (1, row_count - 2, 1), range(first, first + frame_count)
+    )
+
+
+def convolve_rest(field, weights, first, partial, emit):
+    frame_count, row_count = field.shape[0] - 2, field.shape[1] - 2
+    rim = [e for e in range(frame_count + 2) if not first <= e < first + frame_count]
+    convolve(field, weights, emit, (1, row_count - 2, 1), rim, partial)
+    convolve(field, weights, emit, (0, 2, row_count - 1))
 
 
 def kernel_grad(upstream, field, total):
@@ -240,16 +260,45 @@
 
 def block_kernel(
     frames, rows, inv_scale,
-    clip_ref, cot_ref, one_ref, two_ref, bias_ref,
-    block_ref, input_ref, first_ref, second_ref, bias_out_ref,
-    clip_f, cot_f, act_f, pre_f, slope, one_w, two_w, one_adj, two_adj, grad_sum, bias_sum,
+    clip_hbm, cot_hbm, one_hbm, two_hbm, bias_hbm,
+    block_hbm, input_hbm, first_hbm, second_hbm, bias_out_ref,
+    block_ref, input_ref, first_ref, second_ref, out_sems,
+    one_ref, two_ref, bias_ref, local_sems,
+    clip_f, cot_f, act_f, pre_f, slope, grad_act, one_w, two_w, one_adj, two_adj, grad_sum, bias_sum,
     send, got_f, part, total, got_r, full,
     halo_sems, reduce_sems,
 ):
     f, r = lax.axis_index("frames"), lax.axis_index("rows")
-    frame_count, row_count, chan, cols = clip_ref.shape
+    frame_count, row_count, chan, cols = clip_hbm.shape
     place, sizes = (f, r), (frames, rows)
 
+    mid = slice(chan, 2 * chan)
+    inner = pl.ds(1, row_count), pl.ds(chan, chan)
+    loads = [
+        pltpu.make_async_copy(src, dst, local_sems.at[n])
+        for n, (src, dst) in enumerate(
+            (
+                (clip_hbm, clip_f.at[pl.ds(2, frame_count), *inner]),
+                (one_hbm, one_ref),
+                (bias_hbm, bias_ref),
+                (cot_hbm, cot_f.at[pl.ds(0, frame_count), *inner]),
+                (two_hbm, two_ref),
+            )
+        )
+    ]
+    for load in loads:
+        load.start()
+    stores = [
+        pltpu.make_async_copy(src, dst, out_sems.at[n])
+        for n, (src, dst) in enumerate(
+            (
+                (block_ref, block_hbm),
+                (input_ref, input_hbm),
+                (first_ref, first_hbm),
+                (second_ref, second_hbm),
+            )
+        )
+    ]
     barrier = pltpu.get_barrier_semaphore()
     others = [(lax.rem(f + d, frames), r) for d in range(1, frames)]
     others += [(f, lax.rem(r + d, rows)) for d in range(1, rows)]
@@ -258,9 +307,7 @@
             others.append((lax.rem(f + df, frames), lax.rem(r + dr, rows)))
     for device in others:
         pl.semaphore_signal(barrier, inc=1, device_id=device, device_id_type=MESH)
-    mid = slice(chan, 2 * chan)
-    clip_f[2 : frame_count + 2, 1 : row_count + 1, mid] = clip_ref[...]
-    cot_f[0:frame_count, 1 : row_count + 1, mid] = cot_ref[...]
+    loads[0].wait()
     pl.semaphore_wait(barrier, len(others))
 
     clip_h = Halo(clip_f, halo_sems.at[0], False, sizes, place)
@@ -268,11 +315,17 @@
     act_h = Halo(act_f, halo_sems.at[2], False, sizes, place)
     pre_h = Halo(pre_f, halo_sems.at[3], True, sizes, place)
     clip_h.start()
+    loads[1].wait()
     lay_forward(one_ref, one_w)
     clip_h.shift_local()
+    convolve_local(clip_f, one_w, 2, slope)
+    for load in loads[2:]:
+        load.wait()
+    cot_h.start()
+    cot_h.shift_local()
     lay_adjoint(two_ref, two_adj)
+    convolve_local(cot_f, two_adj, 0, grad_act)
     clip_h.receive()
-    cot_h.start()
     clip_h.shift_rim()
 
     def emit_hidden(fr, rr, value):
@@ -281,9 +334,8 @@
         act_f[fr + 2, rr + 1, mid] = (hidden * sig).astype(jnp.bfloat16)
         slope[fr, rr] = sig * (1.0 + hidden * (1.0 - sig))
 
-    convolve(clip_f, one_w, emit_hidden)
+    convolve_rest(clip_f, one_w, 2, slope, emit_hidden)
     act_h.start()
-    cot_h.shift_local()
     act_h.shift_local()
 
     cot_h.receive()
@@ -295,7 +347,7 @@
         pre_f[fr, rr + 1, mid] = pre
         bias_sum[...] += pre.astype(jnp.float32)
 
-    convolve(cot_f, two_adj, emit_pre)
+    convolve_rest(cot_f, two_adj, 0, grad_act, emit_pre)
     pre_h.start()
 
     wide = one_w.shape[1] // LANES
@@ -329,33 +381,36 @@
     act_h.shift_rim()
     kernel_grad(cot_f, act_f, grad_sum)
     reduce_grad(1)
+    reductions[0].scatter_rows()
     lay_forward(two_ref, two_w)
     lay_adjoint(one_ref, one_adj)
     pre_h.shift_local()
 
     def emit_block(fr, rr, value):
-        block_ref[fr, rr] = (clip_ref[fr, rr].astype(jnp.float32) + value).astype(jnp.bfloat16)
+        block_ref[fr, rr] = (clip_f[fr + 2, rr + 1, mid].astype(jnp.float32) + value).astype(jnp.bfloat16)
 
     half_way = row_count // 2
-    convolve(act_f, two_w, emit_block, 0, half_way)
-    reductions[0].scatter_rows()
-    convolve(act_f, two_w, emit_block, half_way, row_count)
+    convolve(act_f, two_w, emit_block, (0, half_way, 1))
+    reductions[0].gather_rows()
+    convolve(act_f, two_w, emit_block, (half_way, 1, 1))
     reductions[1].scatter_rows()
+    convolve(act_f, two_w, emit_block, (half_way + 1, row_count - half_way - 1, 1))
+    stores[0].start()
+    reductions[0].gather_frames()
 
     pre_h.receive()
     pre_h.shift_rim()
 
     def emit_input(fr, rr, value):
-        input_ref[fr, rr] = (cot_ref[fr, rr].astype(jnp.float32) + value).astype(jnp.bfloat16)
-
-    convolve(pre_f, one_adj, emit_input, 0, 1)
-    reductions[0].gather_rows()
+        input_ref[fr, rr] = (cot_f[fr, rr + 1, mid].astype(jnp.float32) + value).astype(jnp.bfloat16)
+
+    convolve(pre_f, one_adj, emit_input, (0, half_way, 1))
     reductions[1].gather_rows()
-    convolve(pre_f, one_adj, emit_input, 1, half_way)
-    reductions[0].gather_frames()
+    convolve(pre_f, one_adj, emit_input, (half_way, 1, 1))
     reductions[1].gather_frames()
-    convolve(pre_f, one_adj, emit_input, half_way, row_count)
-
+    convolve(pre_f, one_adj, emit_input, (half_way + 1, row_count - half_way - 1, 1))
+
+    stores[1].start()
     for k, out in enumerate((first_ref, second_ref)):
         reductions[k].finish()
         for t in range(3):
@@ -366,11 +421,14 @@
                 out[t, tap // 3, tap % 3] = (
                     tile[:, inner : inner + chan].astype(jnp.float32) * inv_scale
                 )
+        stores[2 + k].start()
     bias_out_ref[...] = full[0, pl.ds(used - chan, chan)].astype(jnp.float32) * inv_scale
     for reduction in reductions:
         reduction.drain()
     for halo in (clip_h, cot_h, act_h, pre_h):
         halo.drain()
+    for store in stores:
+        store.wait()
 
 
 def per_device(clip_in, kernel_one, bias_one, kernel_two, cotangent):
@@ -389,6 +447,7 @@
     field = pltpu.VMEM((frame_count + 2, row_count + 2, 3 * chan, cols), bf16)
     weights = pltpu.VMEM((tall, wide * LANES), bf16)
     vmem = pl.BlockSpec(memory_space=pltpu.VMEM)
+    hbm = pl.BlockSpec(memory_space=pltpu.HBM)
     block, grad_input, first, second, bias = pl.pallas_call(
         functools.partial(block_kernel, frames, rows, inv_scale),
         out_shape=(
@@ -398,10 +457,20 @@
             jax.ShapeDtypeStruct(kernel_two.shape, f32),
             jax.ShapeDtypeStruct((chan, LANES), f32),
         ),
-        in_specs=[vmem] * 5,
-        out_specs=(vmem,) * 5,
+        in_specs=[hbm] * 5,
+        out_specs=(hbm,) * 4 + (vmem,),
         scratch_shapes=[
+            pltpu.VMEM(clip_in.shape, bf16),
+            pltpu.VMEM(clip_in.shape, bf16),
+            pltpu.VMEM(kernel_one.shape, f32),
+            pltpu.VMEM(kernel_two.shape, f32),
+            dma((4,)),
+            pltpu.VMEM(kernel_one.shape, bf16),
+            pltpu.VMEM(kernel_two.shape, bf16),
+            pltpu.VMEM((chan, 1), f32),
+            dma((5,)),
             field, field, field, field,
+            pltpu.VMEM(clip_in.shape, f32),
             pltpu.VMEM(clip_in.shape, f32),
             weights, weights, weights, weights,
             pltpu.VMEM((wide * LANES, -(-tall // LANES) * LANES), f32),
@@ -416,7 +485,7 @@
             dma((2, 4, 2, max(frames, rows) - 1)),
         ],
         compiler_params=pltpu.CompilerParams(
-            collective_id=0, has_side_effects=True, vmem_limit_bytes=48 * 1024 * 1024
+            collective_id=0, has_side_effects=True, vmem_limit_bytes=62 * 1024 * 1024
         ),
     )(
         clip_in, cotangent, kernel_one, kernel_two, bias_one.reshape((chan, 1)),

time: 69.3 us -> 67.7 us (0.977)
  local copies, waits for them, and re-layouts: 8.88 us -> 7.96 us
  Pallas kernels: 59.5 us -> 58.7 us
    unnamed x14 -> x12, local copies, waits for them, and re-layouts: 8.16 us -> 5.81 us
    slice x1, local copies, waits for them, and re-layouts: 0.63 us -> 1.44 us  [per_device(): return (block, grad_input, first, second, bias[:, 0])]
    pallas_call x1, Pallas kernels: 59.5 us -> 58.7 us  [per_device(): pl.pallas_call(functools.partial(block_kernel, frames, rows, inv_scale),...]
where the time goes in v4:
time: 67.7 us; the launch traced here: 67.4 us
  Pallas kernels  58.7 us (87%)
  local copies, waits for them, and re-layouts  7.96 us (12%)
    pallas_call x1, Pallas kernels, per_device(): pl.pallas_call(functools.partial(block_kernel, frames, rows, inv_scale),...  58.7 us
    unnamed x12, local copies, waits for them, and re-layouts  5.81 us
    slice x1, local copies, waits for them, and re-layouts, per_device(): return (block, grad_input, first, second, bias[:, 0])  1.44 us

profile of v4, /device:TPU:0, one launch (start us, length us, event | category | flops | bytes accessed | tf_op | source)
XLA Modules:
  0.0 67.4 jit_solution(10535471673580889570)
XLA Ops:
  0.6 0.0 copy-start.3
  0.6 0.6 copy-done.3
  1.3 0.7 %copy.11.bias_hbm = f32[64,1]{1,0:T(8,128)} copy(f32[64,1]{0,1:T(1,128)S(1)} %bitcast.1) | data formatting | bytes 512 | tf_op jit(solution)/shard_map/reshape | solution.py:491
  2.0 58.7 %shard_map.92 = (bf16[4,4,64,256]{3,2,1,0:T(8,128)(2,1)}, bf16[4,4,64,256]{3,2,1,0:T(8,128)(2,1)}, f32[3,3,3,64,64]{4,3,2,1,0:T(8,128)}, f32[3,3,3,64,64]{4,3,2,1,0:T(8,128)}, f32[64,128]{1,0:T(8,128)}) custom-call(bf16[4,4,64,256]{3,2,1,0:T(8,128)(2,1)} %clip_hbm.1, bf16[4,4,64,256]{3,2,1,0:T(8,128)(2,1)} %cot_hbm.1, bf16[3,3,3,64,64]{4,3,2,1,0:T(8,128)(2,1)} %one_hbm.1, ...), custom_call_target="tpu_custom_call" | custom-call | tf_op jit(solution)/shard_map/pallas_call | solution.py:451
  60.8 0.0 copy-start.2
  60.8 1.4 %slice_reduce_fusion = f32[64]{0:T(128)} fusion(f32[64,128]{1,0:T(8,128)} %get-tuple-element.14), kind=kLoop, calls=%fused_computation | loop fusion | bytes 512 | tf_op jit(solution)/shard_map/slice | solution.py:493
  62.2 0.0 copy-start.1
  62.2 2.0 %copy.16 = bf16[4,4,64,256]{3,2,1,0:T(8,128)(2,1)} copy(bf16[4,4,64,256]{3,2,1,0:T(8,128)(2,1)} %get-tuple-element.20) | data formatting | bytes 1048576
  64.2 0.0 copy-done.2
  64.2 0.8 %copy.17 = bf16[4,4,64,256]{3,2,1,0:T(8,128)(2,1)} copy(bf16[4,4,64,256]{3,2,1,0:T(8,128)(2,1)S(1)} %copy-done.2) | data formatting | bytes 1048576
  65.0 0.0 copy-done.1
  65.0 0.0 copy-start
  65.0 0.9 %copy.18 = f32[3,3,3,64,64]{4,3,2,1,0:T(8,128)} copy(f32[3,3,3,64,64]{4,3,2,1,0:T(8,128)S(1)} %copy-done.1) | data formatting | bytes 884736
  65.9 0.6 copy-done
  66.5 0.9 %copy.19 = f32[3,3,3,64,64]{4,3,2,1,0:T(8,128)} copy(f32[3,3,3,64,64]{4,3,2,1,0:T(8,128)S(1)} %copy-done) | data formatting | bytes 884736
Async XLA Ops:
  0.6 0.7 copy-start.3
  60.8 3.4 %copy-start.2 = (bf16[4,4,64,256]{3,2,1,0:T(8,128)(2,1)S(1)}, bf16[4,4,64,256]{3,2,1,0:T(8,128)(2,1)}, u32[]{:S(2)}) copy-start(bf16[4,4,64,256]{3,2,1,0:T(8,128)(2,1)} %get-tuple-element.21) | copy-start | bytes 1572868
  62.2 2.8 %copy-start.1 = (f32[3,3,3,64,64]{4,3,2,1,0:T(8,128)S(1)}, f32[3,3,3,64,64]{4,3,2,1,0:T(8,128)}, u32[]{:S(2)}) copy-start(f32[3,3,3,64,64]{4,3,2,1,0:T(8,128)} %get-tuple-element.22) | copy-start | bytes 1327108
  65.0 1.5 %copy-start = (f32[3,3,3,64,64]{4,3,2,1,0:T(8,128)S(1)}, f32[3,3,3,64,64]{4,3,2,1,0:T(8,128)}, u32[]{:S(2)}) copy-start(f32[3,3,3,64,64]{4,3,2,1,0:T(8,128)} %get-tuple-element.23) | copy-start | bytes 1327108

commit v5 on v4

--- a/solution.py
+++ b/solution.py
@@ -62,13 +62,11 @@
 
         def body(e, carry):
             for row in rows:
-                value = field[e, row, chan : 2 * chan].astype(jnp.float32)
+                value = field[e, row, chan : 2 * chan]
                 cols = value.shape[1]
-                lane = lax.broadcasted_iota(jnp.int32, value.shape, 1)
-                left = jnp.where(lane == 0, 0.0, pltpu.roll(value, 1, 1))
-                right = jnp.where(lane == cols - 1, 0.0, pltpu.roll(value, cols - 1, 1))
-                field[e, row, 0:chan] = left.astype(jnp.bfloat16)
-                field[e, row, 2 * chan : 3 * chan] = right.astype(jnp.bfloat16)
+                blank = jnp.zeros((chan, 1), value.dtype)
+                field[e, row, 0:chan] = jnp.concatenate([blank, value[:, : cols - 1]], axis=1)
+                field[e, row, 2 * chan : 3 * chan] = jnp.concatenate([value[:, 1:], blank], axis=1)
             return carry
 
         lax.fori_loop(first, first + count, body, 0)
@@ -263,7 +261,7 @@
     clip_hbm, cot_hbm, one_hbm, two_hbm, bias_hbm,
     block_hbm, input_hbm, first_hbm, second_hbm, bias_out_ref,
     block_ref, input_ref, first_ref, second_ref, out_sems,
-    one_ref, two_ref, bias_ref, local_sems,
+    one_ref, two_ref, bias_row, bias_ref, local_sems,
     clip_f, cot_f, act_f, pre_f, slope, grad_act, one_w, two_w, one_adj, two_adj, grad_sum, bias_sum,
     send, got_f, part, total, got_r, full,
     halo_sems, reduce_sems,
@@ -280,7 +278,7 @@
             (
                 (clip_hbm, clip_f.at[pl.ds(2, frame_count), *inner]),
                 (one_hbm, one_ref),
-                (bias_hbm, bias_ref),
+                (bias_hbm, bias_row),
                 (cot_hbm, cot_f.at[pl.ds(0, frame_count), *inner]),
                 (two_hbm, two_ref),
             )
@@ -324,6 +322,8 @@
     cot_h.start()
     cot_h.shift_local()
     lay_adjoint(two_ref, two_adj)
+    column = jnp.transpose(jnp.broadcast_to(bias_row[...], (LANES, chan)))[:, 0:1]
+    bias_ref[...] = jnp.broadcast_to(column, bias_ref.shape)
     convolve_local(cot_f, two_adj, 0, grad_act)
     clip_h.receive()
     clip_h.shift_rim()
@@ -422,7 +422,8 @@
                     tile[:, inner : inner + chan].astype(jnp.float32) * inv_scale
                 )
         stores[2 + k].start()
-    bias_out_ref[...] = full[0, pl.ds(used - chan, chan)].astype(jnp.float32) * inv_scale
+    bias_tile = full[0, pl.ds(used - chan, chan)].astype(jnp.float32) * inv_scale
+    bias_out_ref[...] = jnp.transpose(bias_tile)[0:1]
     for reduction in reductions:
         reduction.drain()
     for halo in (clip_h, cot_h, act_h, pre_h):
@@ -455,7 +456,7 @@
             jax.ShapeDtypeStruct(clip_in.shape, bf16),
             jax.ShapeDtypeStruct(kernel_one.shape, f32),
             jax.ShapeDtypeStruct(kernel_two.shape, f32),
-            jax.ShapeDtypeStruct((chan, LANES), f32),
+            jax.ShapeDtypeStruct((1, chan), f32),
         ),
         in_specs=[hbm] * 5,
         out_specs=(hbm,) * 4 + (vmem,),
@@ -467,7 +468,8 @@
             dma((4,)),
             pltpu.VMEM(kernel_one.shape, bf16),
             pltpu.VMEM(kernel_two.shape, bf16),
-            pltpu.VMEM((chan, 1), f32),
+            pltpu.VMEM((1, chan), f32),
+            pltpu.VMEM((chan, cols), f32),
             dma((5,)),
             field, field, field, field,
             pltpu.VMEM(clip_in.shape, f32),
@@ -488,9 +490,9 @@
             collective_id=0, has_side_effects=True, vmem_limit_bytes=62 * 1024 * 1024
         ),
     )(
-        clip_in, cotangent, kernel_one, kernel_two, bias_one.reshape((chan, 1)),
+        clip_in, cotangent, kernel_one, kernel_two, bias_one.reshape((1, chan)),
     )
-    return block, grad_input, first, second, bias[:, 0]
+    return block, grad_input, first, second, bias.reshape((chan,))
 
 
 def solution(mesh):

time: 67.7 us -> 65.3 us (0.965)
  local copies, waits for them, and re-layouts: 7.96 us -> 5.7 us
    slice x1 -> x0, local copies, waits for them, and re-layouts: 1.44 us -> none  [per_device(): return (block, grad_input, first, second, bias[:, 0])]
    reshape x1 -> x0, local copies, waits for them, and re-layouts: 0.71 us -> none  [per_device(): bias_one.reshape((chan, 1))]
    unnamed x12 -> x13, local copies, waits for them, and re-layouts: 5.81 us -> 5.7 us
where the time goes in v5:
time: 65.3 us; the launch traced here: 65 us
  Pallas kernels  58.6 us (90%)
  local copies, waits for them, and re-layouts  5.7 us (9%)
  between operations  0.66 us (1%)
    pallas_call x1, Pallas kernels, per_device(): pl.pallas_call(functools.partial(block_kernel, frames, rows, inv_scale),...  58.6 us
    unnamed x13, local copies, waits for them, and re-layouts  5.7 us

profile of v5, /device:TPU:0, one launch (start us, length us, event | category | flops | bytes accessed | tf_op | source)
XLA Modules:
  0.0 65.0 jit_solution(8938476729738795571)
XLA Ops:
  0.6 58.6 %shard_map.92 = (bf16[4,4,64,256]{3,2,1,0:T(8,128)(2,1)}, bf16[4,4,64,256]{3,2,1,0:T(8,128)(2,1)}, f32[3,3,3,64,64]{4,3,2,1,0:T(8,128)}, f32[3,3,3,64,64]{4,3,2,1,0:T(8,128)}, f32[1,64]{1,0:T(1,128)}) custom-call(bf16[4,4,64,256]{3,2,1,0:T(8,128)(2,1)} %clip_hbm.1, bf16[4,4,64,256]{3,2,1,0:T(8,128)(2,1)} %cot_hbm.1, bf16[3,3,3,64,64]{4,3,2,1,0:T(8,128)(2,1)} %one_hbm.1, ...), custom_call_target="tpu_custom_call" | custom-call | tf_op jit(solution)/shard_map/pallas_call | solution.py:452
  59.3 0.0 copy-start.2
  59.3 0.0 copy-start.1
  59.3 2.0 %copy.15 = bf16[4,4,64,256]{3,2,1,0:T(8,128)(2,1)} copy(bf16[4,4,64,256]{3,2,1,0:T(8,128)(2,1)} %get-tuple-element.20) | data formatting | bytes 1048576
  61.3 0.0 copy-done.2
  61.3 0.8 %copy.16 = bf16[4,4,64,256]{3,2,1,0:T(8,128)(2,1)} copy(bf16[4,4,64,256]{3,2,1,0:T(8,128)(2,1)S(1)} %copy-done.2) | data formatting | bytes 1048576
  62.1 0.0 copy-done.1
  62.1 0.0 copy-start
  62.1 0.9 %copy.17 = f32[3,3,3,64,64]{4,3,2,1,0:T(8,128)} copy(f32[3,3,3,64,64]{4,3,2,1,0:T(8,128)S(1)} %copy-done.1) | data formatting | bytes 884736
  63.0 0.6 copy-done
  63.6 0.0 copy-start.3
  63.6 0.9 %copy.18 = f32[3,3,3,64,64]{4,3,2,1,0:T(8,128)} copy(f32[3,3,3,64,64]{4,3,2,1,0:T(8,128)S(1)} %copy-done) | data formatting | bytes 884736
  64.5 0.0 copy-done.3
  64.5 0.5 copy.19
Async XLA Ops:
  59.3 2.0 %copy-start.2 = (bf16[4,4,64,256]{3,2,1,0:T(8,128)(2,1)S(1)}, bf16[4,4,64,256]{3,2,1,0:T(8,128)(2,1)}, u32[]{:S(2)}) copy-start(bf16[4,4,64,256]{3,2,1,0:T(8,128)(2,1)} %get-tuple-element.21) | copy-start | bytes 1572868
  59.3 2.8 %copy-start.1 = (f32[3,3,3,64,64]{4,3,2,1,0:T(8,128)S(1)}, f32[3,3,3,64,64]{4,3,2,1,0:T(8,128)}, u32[]{:S(2)}) copy-start(f32[3,3,3,64,64]{4,3,2,1,0:T(8,128)} %get-tuple-element.22) | copy-start | bytes 1327108
  62.1 1.5 %copy-start = (f32[3,3,3,64,64]{4,3,2,1,0:T(8,128)S(1)}, f32[3,3,3,64,64]{4,3,2,1,0:T(8,128)}, u32[]{:S(2)}) copy-start(f32[3,3,3,64,64]{4,3,2,1,0:T(8,128)} %get-tuple-element.23) | copy-start | bytes 1327108
  63.6 0.9 %copy-start.3 = (f32[1,64]{1,0:T(1,128)S(1)}, f32[1,64]{1,0:T(1,128)}, u32[]{:S(2)}) copy-start(f32[1,64]{1,0:T(1,128)} %get-tuple-element.14) | copy-start | bytes 772
